TPU v7x, 128 devices: a whole 4x4x4 slice. The times are simulated.
128 devices in a mesh: dp: 8 (over x, y_lo), tensor: 16 (over y_hi, z, core).
Axes of the slice: x: 4, y: 4 (y_hi: 2, y_lo: 2; y = y_hi * 2 + y_lo), z: 4, core: 2. Of those that a mesh axis runs over, the one named last changes fastest.
Arguments:
- tokens: bfloat16 [4096, 2048], P(('dp', 'tensor')), may hold values from -6 to 6
- cotangent: bfloat16 [4096, 2048], P(('dp', 'tensor')), may hold values from -6 to 6
- w_gate: bfloat16 [16, 2048, 5632], P(None, 'dp', 'tensor'), may hold values from -0.125 to 0.125
- w_up: bfloat16 [16, 2048, 5632], P(None, 'dp', 'tensor'), may hold values from -0.125 to 0.125
- w_down: bfloat16 [16, 5632, 2048], P(None, 'tensor', 'dp'), may hold values from -0.078125 to 0.078125
- router: float32 [16, 16], replicated, may hold values from 0 to 1, as said below
Outputs:
- grad_tokens: bfloat16 [4096, 2048], P(('dp', 'tensor'))
- grad_gate: bfloat16 [16, 2048, 5632], P(None, 'dp', 'tensor')
- grad_up: bfloat16 [16, 2048, 5632], P(None, 'dp', 'tensor')
- grad_down: bfloat16 [16, 5632, 2048], P(None, 'tensor', 'dp')
- router_grad: float32 [16, 16], replicated
Inputs may be any that keep to these rules, and one draw needn't show every extreme that they name: `router`: every row is positive and sums to one.
All inputs are finite; a program needn't handle non-finite values.
Results may differ from a plain program's by a relative error of at most 0.0073.
Values may be sent and summed in bfloat16 or wider, within the bound.
A program may use at most 128 MiB of HBM per device.

v0:
```python
import jax
import jax.numpy as jnp
from jax import lax
from jax.sharding import PartitionSpec as P

FF = 5632
SEGLEN = 256


def merge_rows(coeffs, stacked):
    merged = jnp.einsum(
        "se,cedf->csdf",
        coeffs,
        stacked,
        precision=lax.Precision.HIGHEST,
        preferred_element_type=jnp.float32,
    )
    return merged.astype(jnp.bfloat16)


def segment_backward(x_rows, dy_rows, mats):
    mgate = mats[0]
    mup = mats[1]
    mdown_t = mats[2]
    inner = (((0,), (0,)), ((), ()))
    across = (((1,), (1,)), ((), ()))
    g = jnp.dot(x_rows, mgate, preferred_element_type=jnp.float32)
    u = jnp.dot(x_rows, mup, preferred_element_type=jnp.float32)
    sig = jax.nn.sigmoid(g)
    act = g * sig
    h = (act * u).astype(jnp.bfloat16)
    dh = jnp.dot(dy_rows, mdown_t, preferred_element_type=jnp.float32)
    dg = (dh * u * sig * (1.0 + g * (1.0 - sig))).astype(jnp.bfloat16)
    du = (dh * act).astype(jnp.bfloat16)
    pgate = lax.dot_general(x_rows, dg, inner, preferred_element_type=jnp.float32).astype(
        jnp.bfloat16
    )
    pup = lax.dot_general(x_rows, du, inner, preferred_element_type=jnp.float32).astype(
        jnp.bfloat16
    )
    pdown_t = lax.dot_general(dy_rows, h, inner, preferred_element_type=jnp.float32).astype(
        jnp.bfloat16
    )
    dx_part = lax.dot_general(dg, mgate, across, preferred_element_type=jnp.float32)
    dx_part = dx_part + lax.dot_general(du, mup, across, preferred_element_type=jnp.float32)
    return (dx_part, jnp.stack([pgate, pup, pdown_t]))


def reduce_experts(coeffs, grads):
    return jnp.einsum(
        "se,csdf->cedf",
        coeffs,
        grads,
        precision=lax.Precision.HIGHEST,
        preferred_element_type=jnp.float32,
    )


def inner_terms(grads, stacked):
    return jnp.einsum("csdf,cedf->se", grads, stacked, preferred_element_type=jnp.float32)


def body(tokens, cotangent, w_gate, w_up, w_down, router):
    n_data = lax.axis_size("dp")
    seg_local = router.shape[0] // n_data
    experts = router.shape[1]
    whole_x, whole_dy = (
        lax.all_gather(tokens, "tensor", axis=0, tiled=True),
        lax.all_gather(cotangent, "tensor", axis=0, tiled=True),
    )
    seg_rows = whole_x.shape[0] // seg_local
    stacked = jnp.stack([w_gate, w_up, jnp.swapaxes(w_down, 1, 2)])
    grouped = router.reshape(n_data, seg_local, experts)
    dx_parts = []
    partials = []
    totals = jnp.zeros(stacked.shape, jnp.float32)
    for local in range(seg_local):
        coeffs = grouped[:, local]
        merged = lax.all_to_all(
            merge_rows(coeffs, stacked), "dp", split_axis=1, concat_axis=2, tiled=True
        )
        rows = slice(local * seg_rows, (local + 1) * seg_rows)
        dx_part, grads = segment_backward(whole_x[rows], whole_dy[rows], merged[:, 0])
        dx_parts.append(dx_part)
        returned = lax.all_to_all(grads[:, None], "dp", split_axis=2, concat_axis=1, tiled=True)
        totals = totals + reduce_experts(coeffs, returned)
        partials.append(inner_terms(returned, stacked))
    pieces = []
    for local in range(seg_local):
        pieces.append(lax.psum(partials[local], ("dp", "tensor")))
    summed = jnp.stack(pieces, axis=1)
    router_grad = summed.reshape(n_data * seg_local, experts) / jnp.sqrt(jnp.float32(SEGLEN * FF))
    grad_tokens = lax.psum_scatter(
        jnp.concatenate(dx_parts, axis=0), "tensor", scatter_dimension=0, tiled=True
    ).astype(jnp.bfloat16)
    grad_gate = totals[0].astype(jnp.bfloat16)
    grad_up = totals[1].astype(jnp.bfloat16)
    grad_down = jnp.swapaxes(totals[2], 1, 2).astype(jnp.bfloat16)
    return (grad_tokens, grad_gate, grad_up, grad_down, router_grad)


def solution(mesh):
    placed = (
        P(("dp", "tensor"), None),
        P(("dp", "tensor"), None),
        P(None, "dp", "tensor"),
        P(None, "dp", "tensor"),
        P(None, "tensor", "dp"),
        P(),
    )
    return jax.shard_map(
        body,
        mesh=mesh,
        in_specs=placed,
        out_specs=(
            P(("dp", "tensor"), None),
            P(None, "dp", "tensor"),
            P(None, "dp", "tensor"),
            P(None, "tensor", "dp"),
            P(),
        ),
        check_vma=False,
    )
```

profile of v0, /device:TPU:1, one launch (start us, length us, event | category | flops | bytes accessed | tf_op | source)
XLA Modules:
  0.0 486.9 jit_solution(12201072422924858654)
XLA Ops:
  7.2 0.7 all-gather.5.cloned.1.call-update
  7.9 3.6 copy.77
  11.6 3.3 copy_bitcast_fusion.1
  14.9 3.9 convert_bitcast_fusion
  18.9 3.0 copy.44
  21.9 5.9 %all-to-all-start.1 = ((bf16[3,8,256,352]{2,3,0,1:T(8,128)(2,1)}), bf16[3,8,256,352]{2,3,0,1:T(8,128)(2,1)}, u32[]{:S(2)}, u32[]{:S(2)}) async-start(bf16[3,8,256,352]{2,3,0,1:T(8,128)(2,1)} %copy.44), calls=%async_computation.1 | async-start | bytes 8650752 | tf_op jit(solution)/shard_map/all_to_all | solution.py:79
  27.8 0.7 all-gather.3.cloned.1.call-update
  28.5 5.7 %convert_bitcast_fusion.1 = bf16[3,8,256,352]{2,1,3,0:T(8,128)(2,1)S(1)} fusion(f32[8,16,1,1]{1,0,3,2:T(8,128)S(1)} %bitcast.173, bf16[1,16,256,352]{2,1,3,0:T(8,128)(2,1)S(1)} %bitcast.166, bf16[1,16,256,352]{2,1,3,0:T(8,128)(2,1)} %copy-done.11, bf16[1,16,256,352]{2,1,3,0:T(8,128)(2,1)} %copy-done.13), kind=kOutput, calls=%fused_computation.6 | convolution fusion | flops 426049536 | bytes 12976640 | tf_op jit(solution)/shard_map/se,cedf->csdf/dot_general | solution.py:11
  34.2 3.0 copy.40
  37.2 51.3 %all-to-all-done.1 = bf16[3,8,256,352]{2,3,0,1:T(8,128)(2,1)} async-done(((bf16[3,8,256,352]{2,3,0,1:T(8,128)(2,1)}), bf16[3,8,256,352]{2,3,0,1:T(8,128)(2,1)}, u32[]{:S(2)}, u32[]{:S(2)}) %all-to-all-start.1) | async-done | bytes 4325408 | tf_op jit(solution)/shard_map/all_to_all | solution.py:79
  88.4 5.1 %all-to-all-start = ((bf16[3,8,256,352]{2,3,0,1:T(8,128)(2,1)}), bf16[3,8,256,352]{2,3,0,1:T(8,128)(2,1)}, u32[]{:S(2)}, u32[]{:S(2)}) async-start(bf16[3,8,256,352]{2,3,0,1:T(8,128)(2,1)} %copy.40), calls=%async_computation | async-start | bytes 8650752 | tf_op jit(solution)/shard_map/all_to_all | solution.py:79
  93.5 2.5 fusion.26
  96.0 1.3 copy.66
  97.5 1.3 copy.65
  98.8 2.7 convolution_bitcast_fusion
  101.6 2.7 convolution_bitcast_fusion.1
  104.2 56.4 %all-gather.3.cloned.1.call-done = bf16[512,2048]{1,0:T(8,128)(2,1)} async-done(((bf16[32,2048]{1,0:T(8,128)(2,1)}), bf16[512,2048]{1,0:T(8,128)(2,1)}) %all-gather.3.cloned.1.call-update) | async-done | bytes 2097168 | tf_op jit(solution)/shard_map/all_gather | solution.py:69
  160.6 2.4 multiply_convert_fusion.2
  165.5 2.3 maximum_bitcast_fusion.1
  167.8 10.2 %copy.50 = bf16[3,1,2048,352]{3,0,1,2:T(4,128)(2,1)} copy(bf16[3,1,2048,352]{2,3,0,1:T(8,128)(2,1)} %maximum_bitcast_fusion.1) | data formatting | bytes 8650752 | tf_op jit(solution)/shard_map/broadcast_in_dim | solution.py:85
  178.0 4.8 all-to-all-start.3
  182.8 2.5 fusion.25
  188.1 0.6 multiply_convert_fusion.4
  190.4 2.3 maximum_bitcast_fusion
  192.8 10.2 %copy.48 = bf16[3,1,2048,352]{3,0,1,2:T(4,128)(2,1)} copy(bf16[3,1,2048,352]{2,3,0,1:T(8,128)(2,1)} %maximum_bitcast_fusion) | data formatting | bytes 8650752 | tf_op jit(solution)/shard_map/broadcast_in_dim | solution.py:85
  203.0 67.3 %all-to-all-done.3 = bf16[3,1,2048,352]{3,0,1,2:T(4,128)(2,1)} async-done(((bf16[3,1,2048,352]{3,0,1,2:T(4,128)(2,1)}), bf16[3,1,2048,352]{3,0,1,2:T(4,128)(2,1)}, u32[]{:S(2)}, u32[]{:S(2)}) %all-to-all-start.3) | async-done | bytes 4325408 | tf_op jit(solution)/shard_map/all_to_all | solution.py:85
  270.3 4.7 all-to-all-start.2
  275.3 0.7 fusion.29
  276.4 0.7 fusion.28
  277.1 0.7 convolution_add_fusion
  277.9 0.6 copy-done.6
  278.5 0.7 convolution_add_fusion.1
  279.2 2.5 pad_maximum_fusion.1
  281.8 7.7 %copy.61 = bf16[3,8,256,352]{2,1,3,0:T(8,128)(2,1)} copy(bf16[3,8,256,352]{3,0,2,1:T(4,128)(2,1)} %bitcast.36) | data formatting | bytes 8650752 | tf_op jit(solution)/shard_map/all_to_all | solution.py:85
  289.5 72.4 %all-to-all-done.2 = bf16[3,1,2048,352]{3,0,1,2:T(4,128)(2,1)} async-done(((bf16[3,1,2048,352]{3,0,1,2:T(4,128)(2,1)}), bf16[3,1,2048,352]{3,0,1,2:T(4,128)(2,1)}, u32[]{:S(2)}, u32[]{:S(2)}) %all-to-all-start.2) | async-done | bytes 4325408 | tf_op jit(solution)/shard_map/all_to_all | solution.py:85
  361.9 7.8 %copy.60 = bf16[3,8,256,352]{2,1,3,0:T(8,128)(2,1)} copy(bf16[3,8,256,352]{3,0,2,1:T(4,128)(2,1)} %bitcast.26) | data formatting | bytes 8650752 | tf_op jit(solution)/shard_map/all_to_all | solution.py:85
  369.8 5.9 %convolution_bitcast_fusion.6 = f32[8,1,16]{2,0,1:T(8,128)S(1)} fusion(bf16[3,8,256,352]{2,1,3,0:T(8,128)(2,1)} %copy.61, bf16[1,16,256,352]{2,1,3,0:T(8,128)(2,1)S(1)} %bitcast.167, bf16[1,16,256,352]{2,1,3,0:T(8,128)(2,1)} %copy-done.11, bf16[1,16,256,352]{2,1,3,0:T(8,128)(2,1)} %copy-done.13), kind=kOutput, calls=%fused_computation.34 | convolution fusion | flops 77856768 | bytes 12976640 | tf_op jit(solution)/shard_map/csdf,cedf->se/dot_general | solution.py:60
  376.0 0.8 copy-done.14
  376.8 3.2 convolution_bitcast_fusion.7
  380.1 64.7 %all-reduce = (f32[8,1,16]{2,0,1:T(8,128)S(1)}, f32[8,1,16]{2,0,1:T(8,128)S(1)}) all-reduce(f32[8,1,16]{2,0,1:T(8,128)S(1)} %convolution_bitcast_fusion.6, f32[8,1,16]{2,0,1:T(8,128)S(1)} %convolution_bitcast_fusion.7), channel_id=1, replica_groups=mesh['dp'=8,'tensor'=16] {'dp','tensor'}, use_global_device_ids=true, to_apply=%region_2.0 | all-reduce | flops 256 | bytes 2048 | tf_op jit(solution)/shard_map/psum | solution.py:90
  444.7 0.6 copy.52
  445.3 12.3 %fusion.30 = f32[3,256,352,16]{1,3,2,0:T(8,128)} fusion(bf16[3,8,256,352]{2,1,3,0:T(8,128)(2,1)} %copy.60, f32[8,16,1,1]{1,0,3,2:T(8,128)S(1)} %bitcast.174), kind=kOutput, calls=%fused_computation.66 | convolution fusion | flops 415236096 | bytes 21627392 | tf_op jit(solution)/shard_map/se,csdf->cedf/dot_general | solution.py:50
  457.6 12.0 %fusion = bf16[3,16,256,352]{2,1,3,0:T(8,128)(2,1)S(1)} fusion(f32[3,256,352,16]{1,3,2,0:T(8,128)} %fusion.30, bf16[3,8,256,352]{2,1,3,0:T(8,128)(2,1)} %copy.61, f32[8,16,1,1]{1,0,3,2:T(8,128)S(1)} %bitcast.172), kind=kOutput, calls=%fused_computation.2 | convolution fusion | flops 423886848 | bytes 30278144 | tf_op jit(solution)/shard_map/se,csdf->cedf/dot_general | solution.py:50
  469.6 0.9 slice_bitcast_fusion
  470.5 2.7 copy.55
  473.2 2.6 copy.54
  475.8 2.6 copy.53
  478.5 1.6 convert_element_type.92
  (75 shorter events, 8.1 us)
Async XLA Ops:
  7.2 91.7 %all-gather.5.cloned.1.call-start = ((), (), s32[]{:S(2)}) async-start(), calls=%async_computation.6 | async-start | bytes 2228224 | tf_op jit(solution)/shard_map/all_gather | solution.py:68
  7.2 4.3 copy-start.23
  7.9 3.6 copy-start.9
  7.9 3.6 copy-start.10
  11.5 17.0 %copy-start.7 = (bf16[16,352,256]{2,0,1:T(8,128)(2,1)}, bf16[16,352,256]{2,0,1:T(8,128)(2,1)S(1)}, u32[]{:S(2)}) copy-start(bf16[16,352,256]{2,0,1:T(8,128)(2,1)S(1)} %copy.77) | copy-start | bytes 8650756
  14.9 4.0 copy-start.11
  14.9 4.0 copy-start.13
  21.9 66.6 %all-to-all-start.1 = ((bf16[3,8,256,352]{2,3,0,1:T(8,128)(2,1)}), bf16[3,8,256,352]{2,3,0,1:T(8,128)(2,1)}, u32[]{:S(2)}, u32[]{:S(2)}) async-start(bf16[3,8,256,352]{2,3,0,1:T(8,128)(2,1)} %copy.44), calls=%async_computation.1 | async-start | bytes 8650752 | tf_op jit(solution)/shard_map/all_to_all | solution.py:79
  27.7 132.8 %all-gather.3.cloned.1.call-start = ((), (), s32[]{:S(2)}) async-start(), calls=%async_computation.5 | async-start | bytes 2228224 | tf_op jit(solution)/shard_map/all_gather | solution.py:69
  88.4 89.6 %all-to-all-start = ((bf16[3,8,256,352]{2,3,0,1:T(8,128)(2,1)}), bf16[3,8,256,352]{2,3,0,1:T(8,128)(2,1)}, u32[]{:S(2)}, u32[]{:S(2)}) async-start(bf16[3,8,256,352]{2,3,0,1:T(8,128)(2,1)} %copy.40), calls=%async_computation | async-start | bytes 8650752 | tf_op jit(solution)/shard_map/all_to_all | solution.py:79
  98.8 2.7 copy-start.1
  163.0 0.7 copy-start.15
  163.0 1.2 copy-start.17
  163.0 1.7 copy-start.24
  163.0 1.7 copy-start.26
  163.0 1.8 copy-start.27
  178.0 92.3 %all-to-all-start.3 = ((bf16[3,1,2048,352]{3,0,1,2:T(4,128)(2,1)}), bf16[3,1,2048,352]{3,0,1,2:T(4,128)(2,1)}, u32[]{:S(2)}, u32[]{:S(2)}) async-start(bf16[3,1,2048,352]{3,0,1,2:T(4,128)(2,1)} %copy.50), calls=%async_computation.4 | async-start | bytes 12582912 | tf_op jit(solution)/shard_map/all_to_all | solution.py:85
  185.5 1.7 copy-start.5
  185.6 1.3 copy-start.2
  185.8 2.2 copy-start.25
  188.7 1.1 copy-start.19
  188.7 1.1 copy-start.21
  203.0 72.3 %copy-start.18 = (bf16[256,352]{0,1:T(8,128)(2,1)S(1)}, bf16[256,352]{0,1:T(8,128)(2,1)}, u32[]{:S(2)}) copy-start(bf16[256,352]{0,1:T(8,128)(2,1)} %copy-done.17) | copy-start | bytes 540676
  270.3 91.6 %all-to-all-start.2 = ((bf16[3,1,2048,352]{3,0,1,2:T(4,128)(2,1)}), bf16[3,1,2048,352]{3,0,1,2:T(4,128)(2,1)}, u32[]{:S(2)}, u32[]{:S(2)}) async-start(bf16[3,1,2048,352]{3,0,1,2:T(4,128)(2,1)} %copy.48), calls=%async_computation.3 | async-start | bytes 12582912 | tf_op jit(solution)/shard_map/all_to_all | solution.py:85
  275.0 1.4 copy-start.3
  275.0 1.4 copy-start.22
  275.0 2.1 copy-start.16
  275.0 203.4 %reduce-scatter.2.cloned.1.call-start = ((), (), s32[]{:S(2)}) async-start(), calls=%async_computation.7 | async-start | bytes 4456448 | tf_op jit(solution)/shard_map/reduce_scatter | solution.py:93
  275.3 1.8 copy-start.4
  277.1 1.4 copy-start.6
  277.1 1.4 copy-start.20
  361.9 7.8 %copy-start.8 = (bf16[16,352,256]{2,0,1:T(8,128)(2,1)S(1)}, bf16[16,352,256]{2,0,1:T(8,128)(2,1)}, u32[]{:S(2)}) copy-start(bf16[16,352,256]{2,0,1:T(8,128)(2,1)} %copy-done.7) | copy-start | bytes 8650756
  369.7 5.9 %copy-start = (bf16[3,8,256,352]{2,1,3,0:T(8,128)(2,1)S(1)}, bf16[3,8,256,352]{2,1,3,0:T(8,128)(2,1)}, u32[]{:S(2)}) copy-start(bf16[3,8,256,352]{2,1,3,0:T(8,128)(2,1)} %copy.60) | copy-start | bytes 12976132
  369.7 6.3 %copy-start.12 = (bf16[1,16,256,352]{2,1,3,0:T(8,128)(2,1)S(1)}, bf16[1,16,256,352]{2,1,3,0:T(8,128)(2,1)}, u32[]{:S(2)}) copy-start(bf16[1,16,256,352]{2,1,3,0:T(8,128)(2,1)} %copy-done.11) | copy-start | bytes 8650756
  369.7 7.1 %copy-start.14 = (bf16[1,16,256,352]{2,1,3,0:T(8,128)(2,1)S(1)}, bf16[1,16,256,352]{2,1,3,0:T(8,128)(2,1)}, u32[]{:S(2)}) copy-start(bf16[1,16,256,352]{2,1,3,0:T(8,128)(2,1)} %copy-done.13) | copy-start | bytes 8650756
Sparse Core Ops, SparseCore 0:
  10.5 65.5 all-gather.4
  78.6 81.9 all-gather.2
  281.9 105.4 reduce-scatter.1
where the time goes:
time: 497 us; the launch traced here: 487 us
  waiting for transfers between devices  249 us (50%)
  local copies, waits for them, and re-layouts  70.6 us (14%)
  blocking collectives  64.7 us (13%)
  matrix products  58.8 us (12%)
  starting transfers between devices  20.7 us (4%)
  between operations  14.5 us (3%)
  other arithmetic  8.85 us (2%)
    all_to_all x2, waiting for transfers between devices, body(): lax.all_to_all(grads[:, None], 'dp', split_axis=2, concat_axis=1, tiled=T...  140 us
    psum x1, blocking collectives, body(): pieces.append(lax.psum(partials[local], ('dp', 'tensor')))  64.7 us
    all_gather x1, waiting for transfers between devices, body(): lax.all_gather(cotangent, 'tensor', axis=0, tiled=True)  56.4 us
    all_to_all x2, waiting for transfers between devices, body(): lax.all_to_all(merge_rows(coeffs, stacked), 'dp', split_axis=1, concat_ax...  51.3 us
    dot_general x2, matrix products, reduce_experts(): jnp.einsum('se,csdf->cedf', coeffs, grads, precision=lax.Precision.HIGHES...  24.3 us
    broadcast_in_dim x2, local copies, waits for them, and re-layouts, body(): grads[:, None]  20.4 us
    unnamed x66, local copies, waits for them, and re-layouts  18.9 us
    all_to_all x2, local copies, waits for them, and re-layouts, body(): lax.all_to_all(grads[:, None], 'dp', split_axis=2, concat_axis=1, tiled=T...  15.5 us
  transfers between devices with their start and end apart: 7, of which 4 were waited for; matrix products, arithmetic and copies ran while one was open for 27% of the time, Pallas kernels for 0%

commit v1 on v0

v1 whole, which is shorter than its diff:
```python
import functools

import jax
import jax.numpy as jnp
from jax import lax
from jax.experimental import pallas as pl
from jax.experimental.pallas import tpu as pltpu
from jax.sharding import PartitionSpec as P

FF = 5632
SEGLEN = 256
MESH = pl.DeviceIdType.MESH
F32 = jnp.float32
BF16 = jnp.bfloat16
NX = 4
NZ = 4
GROUPS = 8
SEGS = 16
EXPERTS = 16
DS = 256
FS = 352
LANES = 128
ROWS_A = 80
ROWS_B = 96
CUT_A = 48
BASE_B = 2 * ROWS_A
FULL_B = 2 * ROWS_B
BLOCK = 32
PACK = 16

ORDER = (
    ("spread", -1),
    ("a5", 1),
    ("b5", 1),
    ("forward", 0),
    ("a6", 1),
    ("b6", 1),
    ("a2", 0),
    ("b2", 0),
    ("grads", 2),
    ("a3", 0),
    ("b3", 0),
    ("d2", 2),
    ("ea", 0),
    ("eb", 0),
    ("d3", 3),
    ("d4", 3),
)
TICKS = GROUPS + 3


def nn(a, b):
    return jnp.dot(a, b, preferred_element_type=F32)


def dims(a, b, ca, cb):
    return lax.dot_general(a, b, (((ca,), (cb,)), ((), ())), preferred_element_type=F32)


def spread_coeffs(big):
    row = lax.broadcasted_iota(jnp.int32, big.shape, 0)
    col = lax.broadcasted_iota(jnp.int32, big.shape, 1)
    own = jnp.where((row % PACK) == (col % PACK), big, 0.0)
    hi = own.astype(BF16)
    lo = (own - hi.astype(F32)).astype(BF16)
    return hi, lo


def layer_kernel(
    tok, cot, big, wg_in, wu_in, wd_in,
    dx_out, rg_out, pg_out, pu_out, pd_out,
    x, wg, wu, wd, mg, mu, md, khi, klo,
    p, h, ra1, ra2a, ra2b, ra3, rb1, rb2, rb3,
    dx, dxc, dz, rz, dy, ry, fo, outs,
    gsum, ars, arc, arz, ary, ard,
    w_sem, t1_s, t1_r, t2_s, t2_r,
    a_s, a_r, b_s, b_r, d_s, d_r, f_s, f_r, pw, r_s, r_r,
):
    d = lax.axis_index("dp")
    t = lax.axis_index("tensor")
    xi, k = d // 2, d % 2
    yh, z, c = t // 8, (t // 2) % NZ, t % 2
    right = (lax.rem(xi + 1, NX) * 2 + k, t)
    left = (lax.rem(xi + 3, NX) * 2 + k, t)
    across = (xi * 2 + 1 - k, t)
    high = (d, (1 - yh) * 8 + z * 2 + c)
    twin = (d, yh * 8 + z * 2 + 1 - c)
    xp, xm, xo = lax.rem(xi + 1, NX), lax.rem(xi + 3, NX), lax.rem(xi + 2, NX)

    def along_z(o):
        return (d, yh * 8 + lax.rem(z + o, NZ) * 2 + c)

    def along_dp(o):
        return (lax.rem(d + o, GROUPS), t)

    def remote(src, dst, ss, rs, dev):
        return pltpu.make_async_remote_copy(
            src_ref=src, dst_ref=dst, send_sem=ss, recv_sem=rs, device_id=dev, device_id_type=MESH
        )

    loads = [
        pltpu.make_async_copy(src, dst, w_sem.at[i])
        for i, (src, dst) in enumerate(((wg_in, wg), (wu_in, wu), (wd_in, wd)))
    ]
    for load in loads:
        load.start()

    peers = [along_dp(o) for o in range(1, GROUPS)] + [along_z(o) for o in range(1, NZ)] + [high, twin]
    barrier = pltpu.get_barrier_semaphore()
    for peer in peers:
        pl.semaphore_signal(barrier, inc=1, device_id=peer, device_id_type=MESH)
    pl.semaphore_wait(barrier, len(peers))

    def t1_copies(o):
        dest = lax.rem(d + o, GROUPS)
        cols = pl.ds(pl.multiple_of(dest * DS, LANES), DS)
        out = []
        for i, src in enumerate((tok, cot)):
            ref = x.at[i, 2 * d + yh, z, c]
            if o == 0:
                out.append(pltpu.make_async_copy(src.at[:, cols], ref, t1_r.at[i, 0]))
            else:
                out.append(remote(src.at[:, cols], ref, t1_s.at[i, o], t1_r.at[i, o], (dest, t)))
        return out

    for o in (4, 3, 5, 2, 6, 1, 7, 0):
        for copy in t1_copies(o):
            copy.start()

    khi[...], klo[...] = spread_coeffs(big[...])

    def merge(src, dst, rows, cols):
        def step(r, carry):
            at = pl.ds(pl.multiple_of(r * PACK, PACK), PACK)
            rhs = src[:, at, :].reshape(EXPERTS * PACK, cols)
            both = nn(khi[...], rhs) + nn(klo[...], rhs)
            dst[:, at, :] = both.astype(BF16).reshape(SEGS, PACK, cols)
            return carry

        lax.fori_loop(0, rows // PACK, step, 0, unroll=4 if rows == DS else 2)

    def t2_high(q):
        ref = x.at[:, 2 * q + yh, z, c]
        return remote(ref, ref, t2_s.at[0, q], t2_r.at[0, q], high)

    def t2_z(q, o):
        ref = x.at[:, pl.ds(2 * q, 2), z, c]
        return remote(ref, ref, t2_s.at[o, q], t2_r.at[o, q], along_z(o))

    def t2_twin(q):
        ref = x.at[:, pl.ds(2 * q, 2), :, c]
        return remote(ref, ref, t2_s.at[4, q], t2_r.at[4, q], twin)

    loads[0].wait()
    merge(wg, mg, DS, FS)

    def to_high(q, carry):
        o = lax.rem(d - q + GROUPS, GROUPS)
        for i in range(2):
            ref = x.at[i, 2 * q + yh, z, c]
            pltpu.make_async_copy(ref, ref, t1_r.at[i, o]).wait()
        t2_high(q).start()
        return carry

    lax.fori_loop(0, GROUPS, to_high, 0)
    loads[1].wait()
    merge(wu, mu, DS, FS)

    def to_z(q, carry):
        t2_high(q).wait_recv()
        for o in range(1, NZ):
            t2_z(q, o).start()
        return carry

    lax.fori_loop(0, GROUPS, to_z, 0)
    loads[2].wait()
    merge(wd, md, FS, DS)

    mine_a = pl.ds(pl.multiple_of(ROWS_A * k, PACK), ROWS_A)
    mine_a0 = pl.ds(pl.multiple_of(ROWS_A * k, PACK), CUT_A)
    mine_a1 = pl.ds(pl.multiple_of(ROWS_A * k + CUT_A, PACK), ROWS_A - CUT_A)
    theirs_a = pl.ds(pl.multiple_of(ROWS_A * (1 - k), PACK), ROWS_A)
    mine_b = pl.ds(pl.multiple_of(BASE_B + ROWS_B * k, PACK), ROWS_B)
    theirs_b = pl.ds(pl.multiple_of(BASE_B + ROWS_B * (1 - k), PACK), ROWS_B)
    all_b = pl.ds(BASE_B, FULL_B)
    b0 = pl.ds(BASE_B, ROWS_B)
    b1 = pl.ds(BASE_B + ROWS_B, ROWS_B)

    def a_copies(q):
        def cp(i, src, dst, dev):
            return remote(src, dst, a_s.at[i, q], a_r.at[i, q], dev)

        same = lambda i, ref, dev: cp(i, ref, ref, dev)
        return [
            cp(0, p.at[q, :, :, theirs_a, :], ra1.at[q], across),
            cp(1, p.at[q, xo, :, mine_a0, :], ra2a.at[q], right),
            cp(2, p.at[q, xo, :, mine_a1, :], ra2b.at[q], left),
            cp(3, p.at[q, xp, :, mine_a, :], ra3.at[q, 0], right),
            cp(4, p.at[q, xm, :, mine_a, :], ra3.at[q, 1], left),
            same(5, h.at[q, xi, :, mine_a, :], right),
            same(6, h.at[q, xi, :, mine_a, :], left),
            same(7, h.at[q, xm, :, mine_a1, :], right),
            same(8, h.at[q, xp, :, mine_a0, :], left),
            same(9, h.at[q, :, :, mine_a, :], across),
        ]

    def b_copies(q):
        def cp(i, src, dst, dev):
            return remote(src, dst, b_s.at[i, q], b_r.at[i, q], dev)

        same = lambda i, ref, dev: cp(i, ref, ref, dev)
        return [
            cp(0, p.at[q, xo, :, b0, :], rb1.at[q, 0], right),
            cp(1, p.at[q, xo, :, b1, :], rb1.at[q, 1], left),
            cp(2, p.at[q, xp, :, all_b, :], rb2.at[q, 0], right),
            cp(3, p.at[q, xm, :, all_b, :], rb2.at[q, 1], left),
            cp(4, p.at[q, xi, :, theirs_b, :], rb3.at[q], across),
            same(5, h.at[q, xi, :, mine_b, :], across),
            same(6, h.at[q, xi, :, all_b, :], right),
            same(7, h.at[q, xi, :, all_b, :], left),
            same(8, h.at[q, xm, :, b0, :], right),
            same(9, h.at[q, xp, :, b1, :], left),
        ]

    def add(ref, at, other):
        ref[at] = (ref[at].astype(F32) + other.astype(F32)).astype(BF16)

    def matrix(i, s):
        return x[i, s].reshape(SEGLEN, DS)

    def spread(q):
        for o in range(1, NZ):
            t2_z(q, o).wait_recv()
        t2_twin(q).start()

    def forward(q):
        t2_twin(q).wait_recv()
        for seg in range(2):
            s = 2 * q + seg
            xs, dys = matrix(0, s), matrix(1, s)
            for i, part in enumerate((dims(mg[s], xs, 0, 1), dims(mu[s], xs, 0, 1), dims(md[s], dys, 1, 1))):
                part = part.astype(BF16)
                for j in range(2):
                    p[q, 2 * seg + j, i] = part[:, j * LANES : (j + 1) * LANES]
        a_copies(q)[0].start()
        b_copies(q)[0].start()
        b_copies(q)[1].start()

    def a2(q):
        cps = a_copies(q)
        cps[0].wait_recv()
        add(p, (q, slice(None), slice(None), mine_a, slice(None)), ra1[q])
        cps[1].start()
        cps[2].start()

    def b2(q):
        cps = b_copies(q)
        cps[0].wait_recv()
        add(p, (q, xp, slice(None), b0, slice(None)), rb1[q, 0])
        cps[2].start()
        cps[1].wait_recv()
        add(p, (q, xm, slice(None), b1, slice(None)), rb1[q, 1])
        cps[3].start()

    def a3(q):
        cps = a_copies(q)
        cps[1].wait_recv()
        add(p, (q, xp, slice(None), mine_a0, slice(None)), ra2a[q])
        cps[3].start()
        cps[2].wait_recv()
        add(p, (q, xm, slice(None), mine_a1, slice(None)), ra2b[q])
        cps[4].start()

    def b3(q):
        cps = b_copies(q)
        cps[2].wait_recv()
        cps[3].wait_recv()
        at = (q, xi, slice(None), all_b, slice(None))
        p[at] = (p[at].astype(F32) + rb2[q, 0].astype(F32) + rb2[q, 1].astype(F32)).astype(BF16)
        cps[4].start()

    def activate(q, rows, gud):
        g, u, dh = gud
        sig = jax.nn.sigmoid(g)
        act = g * sig
        h[q, xi, 0, rows, :] = (dh * u * sig * (1.0 + g * (1.0 - sig))).astype(BF16)
        h[q, xi, 1, rows, :] = (dh * act).astype(BF16)
        h[q, xi, 2, rows, :] = (act * u).astype(BF16)

    def ea(q):
        cps = a_copies(q)
        cps[3].wait_recv()
        cps[4].wait_recv()
        activate(
            q,
            mine_a,
            [
                p[q, xi, i, mine_a, :].astype(F32) + ra3[q, 0, i].astype(F32) + ra3[q, 1, i].astype(F32)
                for i in range(3)
            ],
        )
        cps[5].start()
        cps[6].start()

    def eb(q):
        cps = b_copies(q)
        cps[4].wait_recv()
        activate(q, mine_b, [p[q, xi, i, mine_b, :].astype(F32) + rb3[q, i].astype(F32) for i in range(3)])
        cps[5].start()

    def a5(q):
        cps = a_copies(q)
        cps[5].wait_recv()
        cps[7].start()
        cps[6].wait_recv()
        cps[8].start()

    def b5(q):
        cps = b_copies(q)
        cps[5].wait_recv()
        cps[6].start()
        cps[7].start()

    def a6(q):
        cps = a_copies(q)
        cps[7].wait_recv()
        cps[8].wait_recv()
        cps[9].start()

    def b6(q):
        cps = b_copies(q)
        cps[6].wait_recv()
        cps[8].start()
        cps[7].wait_recv()
        cps[9].start()

    def keep(q):
        pair = pl.ds(2 * q, 2)
        return [
            pltpu.make_async_copy(src.at[pair], dst.at[pair], pw.at[i, q])
            for i, (src, dst) in enumerate(((mg, pg_out), (mu, pu_out), (md, pd_out)))
        ]

    def d_copies(q):
        def cp(i, src, dst, dev):
            return remote(src, dst, d_s.at[i, q], d_r.at[i, q], dev)

        return (
            [cp(0, dx.at[q, :, :, 1 - c], dxc.at[q], twin)]
            + [cp(o, dz.at[q, :, lax.rem(z + o, NZ)], rz.at[q, o - 1], along_z(o)) for o in range(1, NZ)]
            + [cp(4, dy.at[q], ry.at[q], high)]
        )

    def grads(q):
        a_copies(q)[9].wait_recv()
        b_copies(q)[8].wait_recv()
        b_copies(q)[9].wait_recv()
        parts = []
        for seg in range(2):
            s = 2 * q + seg
            dg, du, hh = (
                jnp.concatenate([h[q, 2 * seg, i], h[q, 2 * seg + 1, i]], axis=1) for i in range(3)
            )
            dxs = dims(dg, mg[s], 0, 1) + dims(du, mu[s], 0, 1)
            dx[q, seg] = dxs.reshape(NZ, 2, BLOCK, DS)
            parts.append((dg, du, hh))
        d_copies(q)[0].start()
        for seg in range(2):
            s = 2 * q + seg
            dg, du, hh = parts[seg]
            xs, dys = matrix(0, s), matrix(1, s)
            mg[s] = dims(xs, dg, 0, 1).astype(BF16)
            mu[s] = dims(xs, du, 0, 1).astype(BF16)
            md[s] = nn(hh, dys).astype(BF16)
        for copy in keep(q):
            copy.start()

    def d2(q):
        cps = d_copies(q)
        cps[0].wait_recv()
        total = dx[q, :, :, c] + dxc[q]
        dx[q, :, :, c] = total
        dz[q] = total.astype(BF16)
        for o in range(1, NZ):
            cps[o].start()

    def d3(q):
        cps = d_copies(q)
        for o in range(1, NZ):
            cps[o].wait_recv()

        def part(which):
            total = dx[q, which, z, c]
            for o in range(NZ - 1):
                total = total + rz[q, o, which].astype(F32)
            return total

        dy[q] = part(1 - yh).astype(BF16)
        cps[4].start()
        dx[q, yh, z, c] = part(yh)

    def final(q):
        o = lax.rem(q - d + GROUPS, GROUPS)
        dst = outs.at[:, pl.ds(pl.multiple_of(d * DS, LANES), DS)]
        return (
            remote(fo.at[q], dst, f_s.at[o], f_r.at[o], (q, t)),
            pltpu.make_async_copy(fo.at[q], dst, f_r.at[o]),
        )

    def d4(q):
        d_copies(q)[4].wait_recv()
        fo[q] = (dx[q, yh, z, c] + ry[q].astype(F32)).astype(BF16)
        away, stay = final(q)

        @pl.when(q != d)
        def _():
            away.start()

        @pl.when(q == d)
        def _():
            stay.start()

    stages = dict(
        spread=spread, forward=forward, a2=a2, b2=b2, a3=a3, b3=b3, ea=ea, eb=eb, a5=a5, b5=b5,
        a6=a6, b6=b6, grads=grads, d2=d2, d3=d3, d4=d4,
    )
    spread(0)

    def tick(n, carry):
        for name, lag in ORDER:
            q = n - lag

            @pl.when((q >= (1 if lag < 0 else 0)) & (q < GROUPS))
            def _(name=name, q=q):
                stages[name](q)

        return carry

    lax.fori_loop(0, TICKS, tick, 0)

    gsum[...] = jnp.zeros_like(gsum)

    def inner(grad, stacked, rows, cols):
        def step(r, carry):
            at = pl.ds(pl.multiple_of(r * PACK, PACK), PACK)
            gsum[...] += dims(
                grad[:, at, :].reshape(SEGS * PACK, cols), stacked[:, at, :].reshape(EXPERTS * PACK, cols), 1, 1
            )
            return carry

        lax.fori_loop(0, rows // PACK, step, 0, unroll=4 if rows == DS else 2)

    inner(mg, wg, DS, FS)
    inner(mu, wu, DS, FS)
    inner(md, wd, FS, DS)
    square = gsum.shape
    row = lax.broadcasted_iota(jnp.int32, square, 0)
    col = lax.broadcasted_iota(jnp.int32, square, 1)
    diag = jnp.where((row % PACK) == (col % PACK), gsum[...], 0.0)
    by_seg = jnp.sum(diag.reshape(SEGS, PACK, EXPERTS * PACK), axis=1)
    pick_row = lax.broadcasted_iota(jnp.int32, (EXPERTS * PACK, LANES), 0)
    pick_col = lax.broadcasted_iota(jnp.int32, (EXPERTS * PACK, LANES), 1)
    pick = jnp.where((pick_row // PACK) == pick_col, 1.0, 0.0).astype(F32)
    own = jnp.dot(by_seg, pick, precision=lax.Precision.HIGHEST, preferred_element_type=F32)

    def r_copies():
        def cp(i, src, dst, dev):
            return remote(src, dst, r_s.at[i], r_r.at[i], dev)

        return (
            [cp(0, ars.at[0], arc, twin)]
            + [cp(o, arz.at[z], arz.at[z], along_z(o)) for o in range(1, NZ)]
            + [cp(4, ars.at[1], ary, high)]
            + [cp(4 + o, ard.at[d], ard.at[d], along_dp(o)) for o in range(1, GROUPS)]
        )

    cps = r_copies()
    ars[0] = own
    cps[0].start()
    cps[0].wait_recv()
    arz[z] = own + arc[...]
    for o in range(1, NZ):
        cps[o].start()
    for o in range(1, NZ):
        cps[o].wait_recv()
    by_z = (arz[0] + arz[1]) + (arz[2] + arz[3])
    ars[1] = by_z
    cps[4].start()
    cps[4].wait_recv()
    ard[d] = by_z + ary[...]
    for o in range(1, GROUPS):
        cps[4 + o].start()
    for o in range(1, GROUPS):
        cps[4 + o].wait_recv()
    total = ((ard[0] + ard[1]) + (ard[2] + ard[3])) + ((ard[4] + ard[5]) + (ard[6] + ard[7]))
    rg_out[...] = total[:, :EXPERTS] / jnp.sqrt(F32(SEGLEN * FF))

    for o in range(GROUPS):
        ref = outs.at[:, pl.ds(0, DS)]
        pltpu.make_async_copy(ref, ref, f_r.at[o]).wait()
    dx_out[...] = outs[...]
    for copy in cps:
        copy.wait_send()
    for o in range(1, GROUPS):
        for copy in t1_copies(o):
            copy.wait_send()

    def drain(q, carry):
        t2_high(q).wait_send()
        for o in range(1, NZ):
            t2_z(q, o).wait_send()
        t2_twin(q).wait_send()
        for copy in a_copies(q) + b_copies(q) + d_copies(q):
            copy.wait_send()
        for copy in keep(q):
            copy.wait()

        @pl.when(q != d)
        def _():
            final(q)[0].wait_send()

        return carry

    lax.fori_loop(0, GROUPS, drain, 0)


def run_layer(tokens, cotangent, w_gate, w_up, w_down, big):
    vm, dma = pltpu.VMEM, pltpu.SemaphoreType.DMA
    any_spec = pl.BlockSpec(memory_space=pl.ANY)
    vm_spec = pl.BlockSpec(memory_space=pltpu.VMEM)
    n, half = GROUPS, FS
    scratch = [
        vm((2, SEGS, NZ, 2, BLOCK, DS), BF16),
        vm((EXPERTS, DS, FS), BF16), vm((EXPERTS, DS, FS), BF16), vm((EXPERTS, FS, DS), BF16),
        vm((SEGS, DS, FS), BF16), vm((SEGS, DS, FS), BF16), vm((SEGS, FS, DS), BF16),
        vm((DS, DS), BF16), vm((DS, DS), BF16),
        vm((n, NX, 3, FS, LANES), BF16), vm((n, NX, 3, FS, LANES), BF16),
        vm((n, NX, 3, ROWS_A, LANES), BF16),
        vm((n, 3, CUT_A, LANES), BF16), vm((n, 3, ROWS_A - CUT_A, LANES), BF16),
        vm((n, 2, 3, ROWS_A, LANES), BF16),
        vm((n, 2, 3, ROWS_B, LANES), BF16), vm((n, 2, 3, FULL_B, LANES), BF16), vm((n, 3, ROWS_B, LANES), BF16),
        vm((n, 2, NZ, 2, BLOCK, DS), F32), vm((n, 2, NZ, BLOCK, DS), F32),
        vm((n, 2, NZ, BLOCK, DS), BF16), vm((n, NZ - 1, 2, BLOCK, DS), BF16),
        vm((n, BLOCK, DS), BF16), vm((n, BLOCK, DS), BF16), vm((n, BLOCK, DS), BF16),
        vm((BLOCK, n * DS), BF16),
        vm((DS, DS), F32),
        vm((2, SEGS, LANES), F32), vm((SEGS, LANES), F32), vm((NZ, SEGS, LANES), F32),
        vm((SEGS, LANES), F32), vm((n, SEGS, LANES), F32),
        dma((3,)), dma((2, n)), dma((2, n)), dma((5, n)), dma((5, n)),
        dma((10, n)), dma((10, n)), dma((10, n)), dma((10, n)),
        dma((5, n)), dma((5, n)), dma((n,)), dma((n,)), dma((3, n)), dma((12,)), dma((12,)),
    ]
    return pl.pallas_call(
        layer_kernel,
        out_shape=(
            jax.ShapeDtypeStruct((BLOCK, n * DS), BF16),
            jax.ShapeDtypeStruct((SEGS, EXPERTS), F32),
            jax.ShapeDtypeStruct((SEGS, DS, FS), BF16),
            jax.ShapeDtypeStruct((SEGS, DS, FS), BF16),
            jax.ShapeDtypeStruct((SEGS, FS, DS), BF16),
        ),
        in_specs=[vm_spec, vm_spec, vm_spec, any_spec, any_spec, any_spec],
        out_specs=[vm_spec, vm_spec, any_spec, any_spec, any_spec],
        scratch_shapes=scratch,
        compiler_params=pltpu.CompilerParams(
            collective_id=0, has_side_effects=True, vmem_limit_bytes=63 * 2**20
        ),
        name="layer_backward",
    )(tokens, cotangent, big, w_gate, w_up, w_down)


def combine_kernel(count, big, *refs):
    srcs, dsts = refs[:count], refs[count : 2 * count]
    khi, klo = refs[2 * count :]

    @pl.when(pl.program_id(0) == 0)
    def _():
        khi[...], klo[...] = spread_coeffs(big[...])

    for src, dst in zip(srcs, dsts):
        cols = src.shape[2]
        for r in range(src.shape[1] // PACK):
            at = pl.ds(r * PACK, PACK)
            rhs = src[:, at, :].reshape(SEGS * PACK, cols)
            both = nn(khi[...], rhs) + nn(klo[...], rhs)
            dst[:, at, :] = both.astype(BF16).reshape(EXPERTS, PACK, cols)


def combine(big, rows, *parts):
    spec = lambda a: pl.BlockSpec((a.shape[0], rows, a.shape[2]), lambda i: (0, i, 0))
    return pl.pallas_call(
        functools.partial(combine_kernel, len(parts)),
        grid=(parts[0].shape[1] // rows,),
        out_shape=[jax.ShapeDtypeStruct(a.shape, BF16) for a in parts],
        in_specs=[pl.BlockSpec(memory_space=pltpu.VMEM)] + [spec(a) for a in parts],
        out_specs=[spec(a) for a in parts],
        scratch_shapes=[pltpu.VMEM((DS, DS), BF16), pltpu.VMEM((DS, DS), BF16)],
        compiler_params=pltpu.CompilerParams(vmem_limit_bytes=32 * 2**20),
        name="combine_experts",
    )(big, *parts)


def body(tokens, cotangent, w_gate, w_up, w_down, router):
    big = jnp.repeat(jnp.repeat(router, PACK, axis=0), PACK, axis=1)
    big_t = jnp.repeat(jnp.repeat(router.T, PACK, axis=0), PACK, axis=1)
    grad_tokens, router_grad, pg, pu, pd = run_layer(tokens, cotangent, w_gate, w_up, w_down, big)
    grad_gate, grad_up = combine(big_t, 32, pg, pu)
    (grad_down,) = combine(big_t, 32, pd)
    return (grad_tokens, grad_gate, grad_up, grad_down, router_grad)


def solution(mesh):
    placed = (
        P(("dp", "tensor"), None),
        P(("dp", "tensor"), None),
        P(None, "dp", "tensor"),
        P(None, "dp", "tensor"),
        P(None, "tensor", "dp"),
        P(),
    )
    return jax.shard_map(
        body,
        mesh=mesh,
        in_specs=placed,
        out_specs=(
            P(("dp", "tensor"), None),
            P(None, "dp", "tensor"),
            P(None, "dp", "tensor"),
            P(None, "tensor", "dp"),
            P(),
        ),
        check_vma=False,
    )
```

time: 497 us -> 275 us (0.55); the launches traced: 487 us -> 274 us
  waiting for transfers between devices: 249 us -> 0 us
  Pallas kernels: 0 us -> 248 us
  blocking collectives: 64.7 us -> 0 us
  matrix products: 58.8 us -> 0 us
  local copies, waits for them, and re-layouts: 70.6 us -> 24.8 us
  starting transfers between devices: 20.7 us -> 0 us
  between operations: 14.5 us -> 0.73 us
  other arithmetic: 8.85 us -> 0 us
    pallas_call x0 -> x3, Pallas kernels: none -> 248 us  [the longest x1 235 us: run_layer(): pl.pallas_call(layer_kernel, out_shape=(jax.ShapeDtypeStruct((BLOCK, n *...]
    all_to_all x4 -> x0, waiting for transfers between devices: 191 us -> none  [the longest x2 140 us: body(): lax.all_to_all(grads[:, None], 'dp', split_axis=2, concat_axis=1, tiled=T...]
    psum x1 -> x0, blocking collectives: 64.7 us -> none  [body(): pieces.append(lax.psum(partials[local], ('dp', 'tensor')))]
    dot_general x22 -> x0, matrix products: 58.8 us -> none  [the longest x2 24.3 us: reduce_experts(): jnp.einsum('se,csdf->cedf', coeffs, grads, precision=lax.Precision.HIGHES...]
    all_gather x2 -> x0, waiting for transfers between devices: 56.4 us -> none  [the longest x1 56.4 us: body(): lax.all_gather(cotangent, 'tensor', axis=0, tiled=True)]
    all_to_all x4 -> x0, starting transfers between devices: 20.4 us -> none  [the longest x2 10.9 us: body(): lax.all_to_all(merge_rows(coeffs, stacked), 'dp', split_axis=1, concat_ax...]
    broadcast_in_dim x2 -> x4, local copies, waits for them, and re-layouts: 20.4 us -> 0.22 us  [the longest x2 0.11 us: body(): big = jnp.repeat(jnp.repeat(router, PACK, axis=0), PACK, axis=1)]
    all_to_all x2 -> x0, local copies, waits for them, and re-layouts: 15.5 us -> none  [body(): lax.all_to_all(grads[:, None], 'dp', split_axis=2, concat_axis=1, tiled=T...]
  transfers between devices with their start and end apart: 7 -> 0, of which waited for: 4 -> 0; matrix products, arithmetic and copies ran while one was open for 27% -> 0% of each run, Pallas kernels for 0% -> 0%
where the time goes in v1:
time: 275 us; the launch traced here: 274 us
  Pallas kernels  248 us (90%)
  local copies, waits for them, and re-layouts  24.8 us (9%)
    pallas_call x1, Pallas kernels, run_layer(): pl.pallas_call(layer_kernel, out_shape=(jax.ShapeDtypeStruct((BLOCK, n *...  235 us
    unnamed x23, local copies, waits for them, and re-layouts  23.4 us
    pallas_call x2, Pallas kernels, combine(): pl.pallas_call(functools.partial(combine_kernel, len(parts)), grid=(parts...  13.2 us

profile of v1, /device:TPU:1, one launch (start us, length us, event | category | flops | bytes accessed | tf_op | source)
XLA Modules:
  0.0 273.9 jit_solution(9153756886547732245)
XLA Ops:
  0.6 0.0 copy-start.4
  0.6 4.7 %copy.18.wg_in = bf16[16,256,352]{2,1,0:T(8,128)(2,1)} copy(bf16[16,256,352]{1,2,0:T(8,128)(2,1)} %param.8) | data formatting | bytes 5767168 | tf_op args[2]
  5.4 0.0 copy-done.4
  5.4 0.0 copy-start.6
  5.4 2.8 %copy.19.wu_in = bf16[16,256,352]{2,1,0:T(8,128)(2,1)} copy(bf16[16,256,352]{1,2,0:T(8,128)(2,1)S(1)} %copy-done.4) | data formatting | bytes 5767168 | tf_op args[3]
  8.2 0.0 copy-done.6
  8.2 0.1 copy.16
  8.2 0.1 broadcast_in_dim.12
  8.3 0.1 reshape.22
  8.5 0.8 copy.17.big
  9.3 235.1 %layer_backward.1 = (bf16[32,2048]{1,0:T(8,128)(2,1)}, f32[16,16]{1,0:T(8,128)}, bf16[16,256,352]{2,1,0:T(8,128)(2,1)}, bf16[16,256,352]{2,1,0:T(8,128)(2,1)}, bf16[16,352,256]{2,1,0:T(8,128)(2,1)}) custom-call(bf16[32,2048]{1,0:T(8,128)(2,1)} %tok.1, bf16[32,2048]{1,0:T(8,128)(2,1)} %cot.1, f32[256,256]{1,0:T(8,128)} %copy.17.big, ...), custom_call_target="tpu_custom_call" | custom-call | tf_op jit(solution)/shard_map/layer_backward/pallas_call | solution.py:553
  244.4 0.1 broadcast_in_dim.14
  244.5 0.1 reshape.24
  244.6 0.1 copy.20.big
  244.8 0.0 copy-start
  244.8 1.9 copy-done
  246.7 0.0 copy-start.1
  246.7 1.9 copy-done.1
  248.5 7.0 %combine_experts.2 = (bf16[16,256,352]{2,1,0:T(8,128)(2,1)S(1)}, bf16[16,256,352]{2,1,0:T(8,128)(2,1)S(1)}) custom-call(f32[256,256]{1,0:T(8,128)S(1)} %copy.20.big, bf16[16,256,352]{2,1,0:T(8,128)(2,1)S(1)} %copy-done, bf16[16,256,352]{2,1,0:T(8,128)(2,1)S(1)} %copy-done.1), custom_call_target="tpu_custom_call" | custom-call | tf_op jit(solution)/shard_map/combine_experts/pallas_call | solution.py:591
  255.6 0.0 copy-start.2
  255.6 1.6 copy-done.2
  257.2 4.6 %copy.22 = bf16[16,256,352]{1,2,0:T(8,128)(2,1)} copy(bf16[16,256,352]{2,1,0:T(8,128)(2,1)} %copy-done.2) | data formatting | bytes 5767168
  261.8 2.8 %copy.23 = bf16[16,256,352]{1,2,0:T(8,128)(2,1)} copy(bf16[16,256,352]{2,1,0:T(8,128)(2,1)S(1)} %get-tuple-element.26) | data formatting | bytes 5767168
  264.6 0.0 copy-start.3
  264.6 1.8 copy-done.3
  266.4 0.0 copy-start.5
  266.4 0.0 copy-start.7
  266.4 6.2 %combine_experts.3 = bf16[16,352,256]{2,1,0:T(8,128)(2,1)} custom-call(f32[256,256]{1,0:T(8,128)S(1)} %copy.20.big, bf16[16,352,256]{2,1,0:T(8,128)(2,1)S(1)} %copy-done.3), custom_call_target="tpu_custom_call" | custom-call | tf_op jit(solution)/shard_map/combine_experts/pallas_call | solution.py:591
  272.6 0.0 copy-done.5
  272.6 0.7 copy.26
  273.3 0.0 copy-done.7
  273.3 0.6 copy.27
  (2 shorter events, 0.0 us)
Async XLA Ops:
  0.6 4.7 %copy-start.4 = (bf16[16,256,352]{1,2,0:T(8,128)(2,1)S(1)}, bf16[16,256,352]{1,2,0:T(8,128)(2,1)}, u32[]{:S(2)}) copy-start(bf16[16,256,352]{1,2,0:T(8,128)(2,1)} %param.9) | copy-start | bytes 8650756
  5.4 2.8 %copy-start.6 = (f32[16,16]{1,0:T(8,128)S(1)}, f32[16,16]{1,0:T(8,128)}, u32[]{:S(2)}) copy-start(f32[16,16]{1,0:T(8,128)} %param.11) | copy-start | bytes 3076
  244.8 1.9 copy-start
  246.7 1.9 copy-start.1
  255.6 1.6 copy-start.2
  264.6 1.8 copy-start.3
  266.4 6.2 %copy-start.5 = (bf16[32,2048]{1,0:T(8,128)(2,1)S(1)}, bf16[32,2048]{1,0:T(8,128)(2,1)}, u32[]{:S(2)}) copy-start(bf16[32,2048]{1,0:T(8,128)(2,1)} %get-tuple-element.34) | copy-start | bytes 393220
  266.4 6.9 %copy-start.7 = (f32[16,16]{1,0:T(8,128)S(1)}, f32[16,16]{1,0:T(8,128)}, u32[]{:S(2)}) copy-start(f32[16,16]{1,0:T(8,128)} %get-tuple-element.38) | copy-start | bytes 3076

commit v2 on v1

v2 whole, which is shorter than its diff:
```python
import functools

import jax
import jax.numpy as jnp
from jax import lax
from jax.experimental import pallas as pl
from jax.experimental.pallas import tpu as pltpu
from jax.sharding import PartitionSpec as P

FF = 5632
SEGLEN = 256
MESH = pl.DeviceIdType.MESH
F32 = jnp.float32
BF16 = jnp.bfloat16
NX = 4
NZ = 4
NT = 16
HALVES = 2
GROUPS = 8
SEGS = 16
EXPERTS = 16
DS = 256
FS = 352
LANES = 128
ROWS_A = 80
ROWS_B = 96
CUT_A = 48
BASE_B = 2 * ROWS_A
FULL_B = 2 * ROWS_B
BLOCK = 32
PACK = 16

ORDER = (
    ("spread", -1),
    ("b3", 6),
    ("a5", 11),
    ("b2", 2),
    ("forward", 0),
    ("a3", 7),
    ("b6", 14),
    ("a6", 13),
    ("ea", 9),
    ("b5", 12),
    ("a2", 4),
    ("grads", 15),
    ("eb", 8),
    ("d2", 16),
    ("d3", 17),
    ("d4", 18),
)
LAST = 15
TAIL = tuple(name for name, lag in ORDER if lag > LAST)
TICKS = GROUPS + LAST


def nn(a, b):
    return jnp.dot(a, b, preferred_element_type=F32)


def dims(a, b, ca, cb):
    return lax.dot_general(a, b, (((ca,), (cb,)), ((), ())), preferred_element_type=F32)


def spread_coeffs(router, by_expert=False):
    wide = (SEGS * PACK, EXPERTS)
    rows = jnp.where(
        lax.broadcasted_iota(jnp.int32, wide, 0) // PACK == lax.broadcasted_iota(jnp.int32, wide, 1), 1.0, 0.0
    )
    exact = dict(precision=lax.Precision.HIGHEST, preferred_element_type=F32)
    tall = lax.dot_general(rows, router, (((1,), (int(by_expert),)), ((), ())), **exact)
    big = lax.dot_general(tall, rows, (((1,), (1,)), ((), ())), **exact)
    row = lax.broadcasted_iota(jnp.int32, big.shape, 0)
    col = lax.broadcasted_iota(jnp.int32, big.shape, 1)
    own = jnp.where((row % PACK) == (col % PACK), big, 0.0)
    hi = own.astype(BF16)
    lo = (own - hi.astype(F32)).astype(BF16)
    return hi, lo


def layer_kernel(
    tok, cot, router, wg_in, wu_in, wd_in,
    dx_out, rg_out, grad_out,
    x, w, m, khi, klo,
    p, h, ra1, ra2a, ra2b, ra3, rb1, rb2, rb3,
    dx, dxc, dz, rz, dy, ry, fo, outs,
    gsum, art, ard,
    w_sem, t1_s, t1_r, t2_s, t2_r,
    a_s, a_r, b_s, b_r, d_s, d_r, f_s, f_r, pw, r_s, r_r,
):
    d = lax.axis_index("dp")
    t = lax.axis_index("tensor")
    xi, k = d // 2, d % 2
    yh, z, c = t // 8, (t // 2) % NZ, t % 2
    right = (lax.rem(xi + 1, NX) * 2 + k, t)
    left = (lax.rem(xi + 3, NX) * 2 + k, t)
    across = (xi * 2 + 1 - k, t)
    high = (d, (1 - yh) * 8 + z * 2 + c)
    twin = (d, yh * 8 + z * 2 + 1 - c)
    xp, xm, xo = lax.rem(xi + 1, NX), lax.rem(xi + 3, NX), lax.rem(xi + 2, NX)

    def along_z(o):
        return (d, yh * 8 + lax.rem(z + o, NZ) * 2 + c)

    def along_t(o):
        return (d, lax.rem(t + o, NT))

    def along_dp(o):
        return (lax.rem(d + o, GROUPS), t)

    def remote(src, dst, ss, rs, dev):
        return pltpu.make_async_remote_copy(
            src_ref=src, dst_ref=dst, send_sem=ss, recv_sem=rs, device_id=dev, device_id_type=MESH
        )

    loads = [
        pltpu.make_async_copy(src, w.at[i], w_sem.at[i])
        for i, src in enumerate((wg_in, wu_in, wd_in))
    ]
    for load in loads:
        load.start()

    peers = [along_dp(o) for o in range(1, GROUPS)] + [along_t(o) for o in range(1, NT)]
    barrier = pltpu.get_barrier_semaphore()
    for peer in peers:
        pl.semaphore_signal(barrier, inc=1, device_id=peer, device_id_type=MESH)
    pl.semaphore_wait(barrier, len(peers))

    def t1_copies(o):
        dest = lax.rem(d + o, GROUPS)
        cols = pl.ds(pl.multiple_of(dest * DS, LANES), DS)
        out = []
        for i, src in enumerate((tok, cot)):
            ref = x.at[i, 2 * d + yh, z, c]
            if o == 0:
                out.append(pltpu.make_async_copy(src.at[:, cols], ref, t1_r.at[i, 0]))
            else:
                out.append(remote(src.at[:, cols], ref, t1_s.at[i, o], t1_r.at[i, o], (dest, t)))
        return out

    for o in (4, 3, 5, 2, 6, 1, 7, 0):
        for copy in t1_copies(o):
            copy.start()

    khi[...], klo[...] = spread_coeffs(router[...])

    def merge(i):
        def step(r, carry):
            at = pl.ds(pl.multiple_of(r * PACK, PACK), PACK)
            rhs = w[i, :, at, :].reshape(EXPERTS * PACK, DS)
            both = nn(khi[...], rhs) + nn(klo[...], rhs)
            m[i, :, at, :] = both.astype(BF16).reshape(SEGS, PACK, DS)
            return carry

        lax.fori_loop(0, FS // PACK, step, 0, unroll=11)

    def t2_high(q):
        ref = x.at[:, 2 * q + yh, z, c]
        return remote(ref, ref, t2_s.at[0, q], t2_r.at[0, q], high)

    def t2_z(q, o):
        ref = x.at[:, pl.ds(2 * q, 2), z, c]
        return remote(ref, ref, t2_s.at[o, q], t2_r.at[o, q], along_z(o))

    def t2_twin(q):
        ref = x.at[:, pl.ds(2 * q, 2), :, c]
        return remote(ref, ref, t2_s.at[4, q], t2_r.at[4, q], twin)

    loads[0].wait()
    merge(0)

    def to_high(q, carry):
        o = lax.rem(d - q + GROUPS, GROUPS)
        for i in range(2):
            ref = x.at[i, 2 * q + yh, z, c]
            pltpu.make_async_copy(ref, ref, t1_r.at[i, o]).wait()
        t2_high(q).start()
        return carry

    lax.fori_loop(0, GROUPS, to_high, 0)
    loads[1].wait()
    merge(1)

    def to_z(q, carry):
        t2_high(q).wait_recv()
        for o in range(1, NZ):
            t2_z(q, o).start()
        return carry

    lax.fori_loop(0, GROUPS, to_z, 0)
    loads[2].wait()
    merge(2)

    mine_a = pl.ds(pl.multiple_of(ROWS_A * k, PACK), ROWS_A)
    mine_a0 = pl.ds(pl.multiple_of(ROWS_A * k, PACK), CUT_A)
    mine_a1 = pl.ds(pl.multiple_of(ROWS_A * k + CUT_A, PACK), ROWS_A - CUT_A)
    theirs_a = pl.ds(pl.multiple_of(ROWS_A * (1 - k), PACK), ROWS_A)
    mine_b = pl.ds(pl.multiple_of(BASE_B + ROWS_B * k, PACK), ROWS_B)
    theirs_b = pl.ds(pl.multiple_of(BASE_B + ROWS_B * (1 - k), PACK), ROWS_B)
    all_b = pl.ds(BASE_B, FULL_B)
    b0 = pl.ds(BASE_B, ROWS_B)
    b1 = pl.ds(BASE_B + ROWS_B, ROWS_B)

    def a_copy(q, which):
        def cp(i, src, dst, dev):
            return remote(src, dst, a_s.at[i, q], a_r.at[i, q], dev)

        same = lambda i, ref, dev: cp(i, ref, ref, dev)
        return [
            lambda: cp(0, p.at[q, :, :, theirs_a, :], ra1.at[q], across),
            lambda: cp(1, p.at[q, xo, :, mine_a0, :], ra2a.at[q], right),
            lambda: cp(2, p.at[q, xo, :, mine_a1, :], ra2b.at[q], left),
            lambda: cp(3, p.at[q, xp, :, mine_a, :], ra3.at[q, 0], right),
            lambda: cp(4, p.at[q, xm, :, mine_a, :], ra3.at[q, 1], left),
            lambda: same(5, h.at[q, xi, :, mine_a, :], right),
            lambda: same(6, h.at[q, xi, :, mine_a, :], left),
            lambda: same(7, h.at[q, xm, :, mine_a1, :], right),
            lambda: same(8, h.at[q, xp, :, mine_a0, :], left),
            lambda: same(9, h.at[q, :, :, mine_a, :], across),
        ][which]()

    def b_copy(q, which):
        def cp(i, src, dst, dev):
            return remote(src, dst, b_s.at[i, q], b_r.at[i, q], dev)

        same = lambda i, ref, dev: cp(i, ref, ref, dev)
        return [
            lambda: cp(0, p.at[q, xo, :, b0, :], rb1.at[q, 0], right),
            lambda: cp(1, p.at[q, xo, :, b1, :], rb1.at[q, 1], left),
            lambda: cp(2, p.at[q, xp, :, all_b, :], rb2.at[q, 0], right),
            lambda: cp(3, p.at[q, xm, :, all_b, :], rb2.at[q, 1], left),
            lambda: cp(4, p.at[q, xi, :, theirs_b, :], rb3.at[q], across),
            lambda: same(5, h.at[q, xi, :, mine_b, :], across),
            lambda: same(6, h.at[q, xi, :, all_b, :], right),
            lambda: same(7, h.at[q, xi, :, all_b, :], left),
            lambda: same(8, h.at[q, xm, :, b0, :], right),
            lambda: same(9, h.at[q, xp, :, b1, :], left),
        ][which]()

    def add(ref, at, other):
        ref[at] = (ref[at].astype(F32) + other.astype(F32)).astype(BF16)

    def matrix(i, s):
        return x[i, s].reshape(SEGLEN, DS)

    def spread(q):
        for o in range(1, NZ):
            t2_z(q, o).wait_recv()
        t2_twin(q).start()

    def forward(q):
        t2_twin(q).wait_recv()
        for seg in range(2):
            s = 2 * q + seg
            xs, dys = matrix(0, s), matrix(1, s)
            for i, rows in enumerate((xs, xs, dys)):
                part = dims(m[i, s], rows, 1, 1).astype(BF16)
                for j in range(2):
                    p[q, 2 * seg + j, i] = part[:, j * LANES : (j + 1) * LANES]
        a_copy(q, 0).start()
        b_copy(q, 0).start()
        b_copy(q, 1).start()

    def a2(q):
        cps = lambda i: a_copy(q, i)
        cps(0).wait_recv()
        add(p, (q, slice(None), slice(None), mine_a, slice(None)), ra1[q])
        cps(1).start()
        cps(2).start()

    def b2(q):
        cps = lambda i: b_copy(q, i)
        cps(0).wait_recv()
        add(p, (q, xp, slice(None), b0, slice(None)), rb1[q, 0])
        cps(2).start()
        cps(1).wait_recv()
        add(p, (q, xm, slice(None), b1, slice(None)), rb1[q, 1])
        cps(3).start()

    def a3(q):
        cps = lambda i: a_copy(q, i)
        cps(1).wait_recv()
        add(p, (q, xp, slice(None), mine_a0, slice(None)), ra2a[q])
        cps(3).start()
        cps(2).wait_recv()
        add(p, (q, xm, slice(None), mine_a1, slice(None)), ra2b[q])
        cps(4).start()

    def b3(q):
        cps = lambda i: b_copy(q, i)
        cps(2).wait_recv()
        cps(3).wait_recv()
        at = (q, xi, slice(None), all_b, slice(None))
        p[at] = (p[at].astype(F32) + rb2[q, 0].astype(F32) + rb2[q, 1].astype(F32)).astype(BF16)
        cps(4).start()

    def activate(q, rows, gud):
        g, u, dh = gud
        sig = jax.nn.sigmoid(g)
        act = g * sig
        h[q, xi, 0, rows, :] = (dh * u * sig * (1.0 + g * (1.0 - sig))).astype(BF16)
        h[q, xi, 1, rows, :] = (dh * act).astype(BF16)
        h[q, xi, 2, rows, :] = (act * u).astype(BF16)

    def ea(q):
        cps = lambda i: a_copy(q, i)
        cps(3).wait_recv()
        cps(4).wait_recv()
        activate(
            q,
            mine_a,
            [
                p[q, xi, i, mine_a, :].astype(F32) + ra3[q, 0, i].astype(F32) + ra3[q, 1, i].astype(F32)
                for i in range(3)
            ],
        )
        cps(5).start()
        cps(6).start()

    def eb(q):
        cps = lambda i: b_copy(q, i)
        cps(4).wait_recv()
        activate(q, mine_b, [p[q, xi, i, mine_b, :].astype(F32) + rb3[q, i].astype(F32) for i in range(3)])
        cps(5).start()

    def a5(q):
        cps = lambda i: a_copy(q, i)
        cps(5).wait_recv()
        cps(7).start()
        cps(6).wait_recv()
        cps(8).start()

    def b5(q):
        cps = lambda i: b_copy(q, i)
        cps(5).wait_recv()
        cps(6).start()
        cps(7).start()

    def a6(q):
        cps = lambda i: a_copy(q, i)
        cps(7).wait_recv()
        cps(8).wait_recv()
        cps(9).start()

    def b6(q):
        cps = lambda i: b_copy(q, i)
        cps(6).wait_recv()
        cps(8).start()
        cps(7).wait_recv()
        cps(9).start()

    def keep(q):
        pair = pl.ds(2 * q, 2)
        return pltpu.make_async_copy(m.at[:, pair], grad_out.at[:, pair], pw.at[q])

    def d_copy(q, i):
        def cp(src, dst, dev):
            return remote(src, dst, d_s.at[i, q], d_r.at[i, q], dev)

        if i == 0:
            return cp(dx.at[q, :, :, 1 - c], dxc.at[q], twin)
        if i == 4:
            return cp(dy.at[q], ry.at[q], high)
        return cp(dz.at[q, :, lax.rem(z + i, NZ)], rz.at[q, i - 1], along_z(i))

    def grads(q):
        a_copy(q, 9).wait_recv()
        b_copy(q, 8).wait_recv()
        b_copy(q, 9).wait_recv()
        parts = []
        for seg in range(2):
            s = 2 * q + seg
            dg, du, hh = (
                jnp.concatenate([h[q, 2 * seg, i], h[q, 2 * seg + 1, i]], axis=1) for i in range(3)
            )
            dxs = dims(dg, m[0, s], 0, 0) + dims(du, m[1, s], 0, 0)
            dx[q, seg] = dxs.reshape(NZ, 2, BLOCK, DS)
            parts.append((dg, du, hh))
        d_copy(q, 0).start()
        for seg in range(2):
            s = 2 * q + seg
            dg, du, hh = parts[seg]
            xs, dys = matrix(0, s), matrix(1, s)
            m[0, s] = nn(dg, xs).astype(BF16)
            m[1, s] = nn(du, xs).astype(BF16)
            m[2, s] = nn(hh, dys).astype(BF16)
        keep(q).start()

    def d2(q):
        cps = lambda i: d_copy(q, i)
        cps(0).wait_recv()
        total = dx[q, :, :, c] + dxc[q]
        dx[q, :, :, c] = total
        dz[q] = total.astype(BF16)
        for o in range(1, NZ):
            cps(o).start()

    def d3(q):
        cps = lambda i: d_copy(q, i)
        for o in range(1, NZ):
            cps(o).wait_recv()

        def part(which):
            total = dx[q, which, z, c]
            for o in range(NZ - 1):
                total = total + rz[q, o, which].astype(F32)
            return total

        dy[q] = part(1 - yh).astype(BF16)
        cps(4).start()
        dx[q, yh, z, c] = part(yh)

    def final(q, away):
        o = lax.rem(q - d + GROUPS, GROUPS)
        dst = outs.at[:, pl.ds(pl.multiple_of(d * DS, LANES), DS)]
        if away:
            return remote(fo.at[q], dst, f_s.at[o], f_r.at[o], (q, t))
        return pltpu.make_async_copy(fo.at[q], dst, f_r.at[o])

    def d4(q):
        d_copy(q, 4).wait_recv()
        fo[q] = (dx[q, yh, z, c] + ry[q].astype(F32)).astype(BF16)

        @pl.when(q != d)
        def _():
            final(q, True).start()

        @pl.when(q == d)
        def _():
            final(q, False).start()

    stages = dict(
        spread=spread, forward=forward, a2=a2, b2=b2, a3=a3, b3=b3, ea=ea, eb=eb, a5=a5, b5=b5,
        a6=a6, b6=b6, grads=grads, d2=d2, d3=d3, d4=d4,
    )
    spread(0)

    def tick(n, carry):
        for name, lag in ORDER:
            q = n - lag

            @pl.when((q >= (1 if lag < 0 else 0)) & (q < GROUPS))
            def _(name=name, q=q):
                stages[name](q)

        return carry

    lax.fori_loop(0, TICKS, tick, 0)

    gsum[...] = jnp.zeros_like(gsum)

    def inner(i):
        def step(r, carry):
            at = pl.ds(pl.multiple_of(r * PACK, PACK), PACK)
            gsum[...] += dims(
                m[i, :, at, :].reshape(SEGS * PACK, DS), w[i, :, at, :].reshape(EXPERTS * PACK, DS), 1, 1
            )
            return carry

        lax.fori_loop(0, FS // PACK, step, 0, unroll=11)

    inner(0)
    d2(GROUPS - 1)
    d3(GROUPS - 2)
    d4(GROUPS - 3)
    inner(1)
    d3(GROUPS - 1)
    d4(GROUPS - 2)
    inner(2)
    square = gsum.shape
    row = lax.broadcasted_iota(jnp.int32, square, 0)
    col = lax.broadcasted_iota(jnp.int32, square, 1)
    diag = jnp.where((row % PACK) == (col % PACK), gsum[...], 0.0)
    by_seg = jnp.sum(diag.reshape(SEGS, PACK, EXPERTS * PACK), axis=1)
    pick_row = lax.broadcasted_iota(jnp.int32, (EXPERTS * PACK, LANES), 0)
    pick_col = lax.broadcasted_iota(jnp.int32, (EXPERTS * PACK, LANES), 1)
    pick = jnp.where((pick_row // PACK) == pick_col, 1.0, 0.0).astype(F32)
    own = jnp.dot(by_seg, pick, precision=lax.Precision.HIGHEST, preferred_element_type=F32)

    def r_copy(i):
        def cp(ref, dev):
            return remote(ref, ref, r_s.at[i], r_r.at[i], dev)

        if i < NT:
            return cp(art.at[t], along_t(i))
        return cp(ard.at[d], along_dp(i - NT + 1))

    art[t] = own
    for o in range(1, NT):
        r_copy(o).start()
    d4(GROUPS - 1)
    for o in range(1, NT):
        r_copy(o).wait_recv()
    ard[d] = jnp.sum(art[...], axis=0)
    for o in range(1, GROUPS):
        r_copy(NT + o - 1).start()
    for o in range(1, GROUPS):
        r_copy(NT + o - 1).wait_recv()
    total = ((ard[0] + ard[1]) + (ard[2] + ard[3])) + ((ard[4] + ard[5]) + (ard[6] + ard[7]))
    rg_out[...] = total[:, :EXPERTS] / jnp.sqrt(F32(SEGLEN * FF))

    for o in range(GROUPS):
        ref = outs.at[:, pl.ds(0, DS)]
        pltpu.make_async_copy(ref, ref, f_r.at[o]).wait()
    dx_out[...] = outs[...]
    for i in range(1, NT + GROUPS - 1):
        r_copy(i).wait_send()
    for o in range(1, GROUPS):
        for copy in t1_copies(o):
            copy.wait_send()

    def drain(q, carry):
        t2_high(q).wait_send()
        for o in range(1, NZ):
            t2_z(q, o).wait_send()
        t2_twin(q).wait_send()
        for i in range(10):
            a_copy(q, i).wait_send()
            b_copy(q, i).wait_send()
        for i in range(5):
            d_copy(q, i).wait_send()
        keep(q).wait()

        @pl.when(q != d)
        def _():
            final(q, True).wait_send()

        return carry

    lax.fori_loop(0, GROUPS, drain, 0)


def run_layer(tokens, cotangent, w_gate, w_up, w_down, router):
    vm, dma = pltpu.VMEM, pltpu.SemaphoreType.DMA
    any_spec = pl.BlockSpec(memory_space=pl.ANY)
    vm_spec = pl.BlockSpec(memory_space=pltpu.VMEM)
    n = GROUPS
    stacked = (3, SEGS, FS, DS)
    scratch = [
        vm((2, SEGS, NZ, 2, BLOCK, DS), BF16),
        vm((3, EXPERTS, FS, DS), BF16), vm(stacked, BF16),
        vm((DS, DS), BF16), vm((DS, DS), BF16),
        vm((n, NX, 3, FS, LANES), BF16), vm((n, NX, 3, FS, LANES), BF16),
        vm((n, NX, 3, ROWS_A, LANES), BF16),
        vm((n, 3, CUT_A, LANES), BF16), vm((n, 3, ROWS_A - CUT_A, LANES), BF16),
        vm((n, 2, 3, ROWS_A, LANES), BF16),
        vm((n, 2, 3, ROWS_B, LANES), BF16), vm((n, 2, 3, FULL_B, LANES), BF16), vm((n, 3, ROWS_B, LANES), BF16),
        vm((n, 2, NZ, 2, BLOCK, DS), F32), vm((n, 2, NZ, BLOCK, DS), F32),
        vm((n, 2, NZ, BLOCK, DS), BF16), vm((n, NZ - 1, 2, BLOCK, DS), BF16),
        vm((n, BLOCK, DS), BF16), vm((n, BLOCK, DS), BF16), vm((n, BLOCK, DS), BF16),
        vm((BLOCK, n * DS), BF16),
        vm((DS, DS), F32),
        vm((NT, SEGS, LANES), F32), vm((n, SEGS, LANES), F32),
        dma((3,)), dma((2, n)), dma((2, n)), dma((5, n)), dma((5, n)),
        dma((10, n)), dma((10, n)), dma((10, n)), dma((10, n)),
        dma((5, n)), dma((5, n)), dma((n,)), dma((n,)), dma((n,)), dma((NT + n - 1,)), dma((NT + n - 1,)),
    ]
    return pl.pallas_call(
        layer_kernel,
        out_shape=(
            jax.ShapeDtypeStruct((BLOCK, n * DS), BF16),
            jax.ShapeDtypeStruct((SEGS, EXPERTS), F32),
            jax.ShapeDtypeStruct(stacked, BF16),
        ),
        in_specs=[vm_spec, vm_spec, vm_spec, any_spec, any_spec, any_spec],
        out_specs=[vm_spec, vm_spec, any_spec],
        scratch_shapes=scratch,
        compiler_params=pltpu.CompilerParams(
            collective_id=0, has_side_effects=True, vmem_limit_bytes=63 * 2**20
        ),
        name="layer_backward",
    )(tokens, cotangent, router, w_gate, w_up, w_down)


def combine_kernel(router, src, dx_in, rg_in, gate, up, down, dx_out, rg_out, got, made, khi, klo, in_sem, out_sem, pass_sem):
    rows = FS // HALVES
    chunks = [(i, pl.ds(j * rows, rows)) for i in range(3) for j in range(HALVES)]
    ins = [pltpu.make_async_copy(src.at[i, :, at], got.at[n], in_sem.at[n]) for n, (i, at) in enumerate(chunks)]
    outs = [
        pltpu.make_async_copy(made.at[n], (gate, up, down)[i].at[:, at], out_sem.at[n])
        for n, (i, at) in enumerate(chunks)
    ]
    passed = [
        pltpu.make_async_copy(dx_in, dx_out, pass_sem.at[0]),
        pltpu.make_async_copy(rg_in, rg_out, pass_sem.at[1]),
    ]
    for copy in ins + passed:
        copy.start()
    khi[...], klo[...] = spread_coeffs(router[...], by_expert=True)
    for n in range(len(chunks)):
        ins[n].wait()

        def step(r, carry, n=n):
            at = pl.ds(pl.multiple_of(r * PACK, PACK), PACK)
            rhs = got[n, :, at, :].reshape(SEGS * PACK, DS)
            both = nn(khi[...], rhs) + nn(klo[...], rhs)
            made[n, :, at, :] = both.astype(BF16).reshape(EXPERTS, PACK, DS)
            return carry

        lax.fori_loop(0, rows // PACK, step, 0, unroll=11)
        outs[n].start()
    for copy in outs + passed:
        copy.wait()


def combine(router, grads, grad_tokens, router_grad):
    any_spec = pl.BlockSpec(memory_space=pl.ANY)
    n = 3 * HALVES
    like = lambda a: jax.ShapeDtypeStruct(a.shape, a.dtype)
    return pl.pallas_call(
        combine_kernel,
        out_shape=[jax.ShapeDtypeStruct((EXPERTS, FS, DS), BF16)] * 3 + [like(grad_tokens), like(router_grad)],
        in_specs=[pl.BlockSpec(memory_space=pltpu.VMEM)] + [any_spec] * 3,
        out_specs=[any_spec] * 5,
        scratch_shapes=[pltpu.VMEM((n, SEGS, FS // HALVES, DS), BF16)] * 2
        + [pltpu.VMEM((DS, DS), BF16)] * 2
        + [pltpu.SemaphoreType.DMA((n,)), pltpu.SemaphoreType.DMA((n,)), pltpu.SemaphoreType.DMA((2,))],
        compiler_params=pltpu.CompilerParams(vmem_limit_bytes=60 * 2**20),
        name="combine_experts",
    )(router, grads, grad_tokens, router_grad)


def body(tokens, cotangent, w_gate, w_up, w_down, router):
    flip = lambda a: jnp.swapaxes(a, 1, 2)
    grad_tokens, router_grad, grads = run_layer(
        tokens, cotangent, flip(w_gate), flip(w_up), w_down, router
    )
    grad_gate, grad_up, grad_down, grad_tokens, router_grad = combine(router, grads, grad_tokens, router_grad)
    return (grad_tokens, flip(grad_gate), flip(grad_up), grad_down, router_grad)


def solution(mesh):
    placed = (
        P(("dp", "tensor"), None),
        P(("dp", "tensor"), None),
        P(None, "dp", "tensor"),
        P(None, "dp", "tensor"),
        P(None, "tensor", "dp"),
        P(),
    )
    return jax.shard_map(
        body,
        mesh=mesh,
        in_specs=placed,
        out_specs=(
            P(("dp", "tensor"), None),
            P(None, "dp", "tensor"),
            P(None, "dp", "tensor"),
            P(None, "tensor", "dp"),
            P(),
        ),
        check_vma=False,
    )
```

time: 275 us -> 176 us (0.64)
  Pallas kernels: 248 us -> 175 us
  local copies, waits for them, and re-layouts: 24.8 us -> 0 us
    pallas_call x1, Pallas kernels: 235 us -> 166 us  [run_layer(): pl.pallas_call(layer_kernel, out_shape=(jax.ShapeDtypeStruct((BLOCK, n *...]
    unnamed x23 -> x0, local copies, waits for them, and re-layouts: 23.4 us -> none
    pallas_call x2 -> x1, Pallas kernels: 13.2 us -> 9.21 us  [combine(): pl.pallas_call(combine_kernel, out_shape=[jax.ShapeDtypeStruct((EXPERTS,...]
where the time goes in v2:
time: 176 us
  Pallas kernels  175 us (99%)
    pallas_call x1, Pallas kernels, run_layer(): pl.pallas_call(layer_kernel, out_shape=(jax.ShapeDtypeStruct((BLOCK, n *...  166 us
    pallas_call x1, Pallas kernels, combine(): pl.pallas_call(combine_kernel, out_shape=[jax.ShapeDtypeStruct((EXPERTS,...  9.21 us

profile of v2, /device:TPU:1, one launch (start us, length us, event | category | flops | bytes accessed | tf_op | source)
XLA Modules:
  0.0 176.1 jit_solution(12664077174903386973)
XLA Ops:
  0.6 166.1 %layer_backward.1 = (bf16[32,2048]{1,0:T(8,128)(2,1)}, f32[16,16]{1,0:T(8,128)}, bf16[3,16,352,256]{3,2,1,0:T(8,128)(2,1)}) custom-call(bf16[32,2048]{1,0:T(8,128)(2,1)} %tok.1, bf16[32,2048]{1,0:T(8,128)(2,1)} %cot.1, f32[16,16]{1,0:T(8,128)} %router.3, bf16[16,352,256]{2,1,0:T(8,128)(2,1)} %bitcast.4, bf16[16,352,256]{2,1,0:T(8,128)(2,1)} %bitcast.5, ...), custom_call_target="tpu_custom_call" | custom-call | tf_op jit(solution)/shard_map/layer_backward/pallas_call | solution.py:557
  166.7 9.2 %combine_experts.1 = (bf16[16,352,256]{2,1,0:T(8,128)(2,1)}, bf16[16,352,256]{2,1,0:T(8,128)(2,1)}, bf16[16,352,256]{2,1,0:T(8,128)(2,1)}, bf16[32,2048]{1,0:T(8,128)(2,1)}, f32[16,16]{1,0:T(8,128)}) custom-call(f32[16,16]{1,0:T(8,128)} %router.3, bf16[3,16,352,256]{3,2,1,0:T(8,128)(2,1)} %get-tuple-element.13.src, ...), custom_call_target="tpu_custom_call" | custom-call | tf_op jit(solution)/shard_map/combine_experts/pallas_call | solution.py:609

commit v3 on v2

--- a/solution.py
+++ b/solution.py
@@ -17,6 +17,7 @@
 NT = 16
 HALVES = 2
 GROUPS = 8
+OWN = 4
 SEGS = 16
 EXPERTS = 16
 DS = 256
@@ -27,29 +28,42 @@
 CUT_A = 48
 BASE_B = 2 * ROWS_A
 FULL_B = 2 * ROWS_B
+BACK_A = 64
+BACK_B = 112
+SWAP = ROWS_A - BACK_A
+CUT_BACK = 32
+BASE_BACK = 2 * BACK_A
+FULL_BACK = 2 * BACK_B
+PLACES = (
+    (0, 0, BACK_A),
+    (BACK_A, BASE_BACK, SWAP),
+    (ROWS_A, BACK_A, BACK_A),
+    (ROWS_A + BACK_A, BASE_BACK + BACK_B, SWAP),
+    (BASE_B, BASE_BACK + SWAP, ROWS_B),
+    (BASE_B + ROWS_B, BASE_BACK + BACK_B + SWAP, ROWS_B),
+)
 BLOCK = 32
 PACK = 16
 
 ORDER = (
     ("spread", -1),
     ("b3", 6),
-    ("a5", 11),
-    ("b2", 2),
+    ("a2", 3),
+    ("grads", 13),
     ("forward", 0),
-    ("a3", 7),
-    ("b6", 14),
-    ("a6", 13),
-    ("ea", 9),
-    ("b5", 12),
-    ("a2", 4),
-    ("grads", 15),
+    ("a6", 11),
+    ("a5", 10),
     ("eb", 8),
-    ("d2", 16),
-    ("d3", 17),
-    ("d4", 18),
+    ("b2", 1),
+    ("ea", 8),
+    ("b5", 10),
+    ("a3", 4),
+    ("b6", 11),
+    ("d2", 14),
+    ("d3", 15),
+    ("d4", 16),
 )
-LAST = 15
-TAIL = tuple(name for name, lag in ORDER if lag > LAST)
+LAST = 13
 TICKS = GROUPS + LAST
 
 
@@ -78,9 +92,9 @@
 
 
 def layer_kernel(
-    tok, cot, router, wg_in, wu_in, wd_in,
+    tok_in, cot_in, router_in, wg_in, wu_in, wd_in,
     dx_out, rg_out, grad_out,
-    x, w, m, khi, klo,
+    rows_in, router, x, w, m, khi, klo,
     p, h, ra1, ra2a, ra2b, ra3, rb1, rb2, rb3,
     dx, dxc, dz, rz, dy, ry, fo, outs,
     gsum, art, ard,
@@ -116,31 +130,28 @@
         pltpu.make_async_copy(src, w.at[i], w_sem.at[i])
         for i, src in enumerate((wg_in, wu_in, wd_in))
     ]
-    for load in loads:
-        load.start()
-
-    peers = [along_dp(o) for o in range(1, GROUPS)] + [along_t(o) for o in range(1, NT)]
+    loads += [
+        pltpu.make_async_copy(tok_in, rows_in.at[0], w_sem.at[3]),
+        pltpu.make_async_copy(cot_in, rows_in.at[1], w_sem.at[4]),
+        pltpu.make_async_copy(router_in, router, w_sem.at[5]),
+    ]
+    for i in (5, 0, 3, 4, 1, 2):
+        loads[i].start()
+
+    peers = [along_dp(o) for o in range(1, GROUPS)] + [along_z(o) for o in range(1, NZ)] + [high, twin]
     barrier = pltpu.get_barrier_semaphore()
     for peer in peers:
         pl.semaphore_signal(barrier, inc=1, device_id=peer, device_id_type=MESH)
-    pl.semaphore_wait(barrier, len(peers))
-
-    def t1_copies(o):
+
+    def t1_copy(o):
         dest = lax.rem(d + o, GROUPS)
         cols = pl.ds(pl.multiple_of(dest * DS, LANES), DS)
-        out = []
-        for i, src in enumerate((tok, cot)):
-            ref = x.at[i, 2 * d + yh, z, c]
-            if o == 0:
-                out.append(pltpu.make_async_copy(src.at[:, cols], ref, t1_r.at[i, 0]))
-            else:
-                out.append(remote(src.at[:, cols], ref, t1_s.at[i, o], t1_r.at[i, o], (dest, t)))
-        return out
-
-    for o in (4, 3, 5, 2, 6, 1, 7, 0):
-        for copy in t1_copies(o):
-            copy.start()
-
+        src, dst = rows_in.at[:, :, cols], x.at[:, d, yh, z, c]
+        if o == 0:
+            return pltpu.make_async_copy(src, dst, t1_r.at[0])
+        return remote(src, dst, t1_s.at[o], t1_r.at[o], (dest, t))
+
+    loads[5].wait()
     khi[...], klo[...] = spread_coeffs(router[...])
 
     def merge(i):
@@ -153,42 +164,56 @@
 
         lax.fori_loop(0, FS // PACK, step, 0, unroll=11)
 
-    def t2_high(q):
-        ref = x.at[:, 2 * q + yh, z, c]
-        return remote(ref, ref, t2_s.at[0, q], t2_r.at[0, q], high)
-
-    def t2_z(q, o):
-        ref = x.at[:, pl.ds(2 * q, 2), z, c]
-        return remote(ref, ref, t2_s.at[o, q], t2_r.at[o, q], along_z(o))
-
-    def t2_twin(q):
-        ref = x.at[:, pl.ds(2 * q, 2), :, c]
-        return remote(ref, ref, t2_s.at[4, q], t2_r.at[4, q], twin)
-
     loads[0].wait()
     merge(0)
-
-    def to_high(q, carry):
-        o = lax.rem(d - q + GROUPS, GROUPS)
+    pl.semaphore_wait(barrier, len(peers))
+    loads[3].wait()
+    loads[4].wait()
+    for o in (4, 3, 5, 2, 6, 1, 7, 0):
+        t1_copy(o).start()
+    for i in (1, 2):
+        loads[i].wait()
+        merge(i)
+
+    def group(q):
+        return 2 * lax.rem(q, OWN), lax.rem(yh + q // OWN, 2)
+
+    def segment(q, i):
+        first, which = group(q)
+        return 2 * (first + i) + which
+
+    def t2_high(a):
+        ref = x.at[:, pl.ds(2 * a, 2), yh, z, c]
+        return remote(ref, ref, t2_s.at[0, a], t2_r.at[0, a], high)
+
+    def t2_z(q, o):
+        first, which = group(q)
+        ref = x.at[:, pl.ds(first, 2), which, z, c]
+        return remote(ref, ref, t2_s.at[o, q], t2_r.at[o, q], along_z(o))
+
+    def t2_twin(q):
+        first, which = group(q)
+        ref = x.at[:, pl.ds(first, 2), which, :, c]
+        return remote(ref, ref, t2_s.at[4, q], t2_r.at[4, q], twin)
+
+    def hand_on(a, carry):
         for i in range(2):
-            ref = x.at[i, 2 * q + yh, z, c]
-            pltpu.make_async_copy(ref, ref, t1_r.at[i, o]).wait()
-        t2_high(q).start()
+            o = lax.rem(d - 2 * a - i + GROUPS, GROUPS)
+            ref = x.at[:, 2 * a + i, yh, z, c]
+            pltpu.make_async_copy(ref, ref, t1_r.at[o]).wait()
+        for o in (2, 1, 3):
+            t2_z(a, o).start()
+        t2_high(a).start()
         return carry
 
-    lax.fori_loop(0, GROUPS, to_high, 0)
-    loads[1].wait()
-    merge(1)
-
-    def to_z(q, carry):
-        t2_high(q).wait_recv()
-        for o in range(1, NZ):
-            t2_z(q, o).start()
+    def hand_on_other(a, carry):
+        t2_high(a).wait_recv()
+        for o in (2, 1, 3):
+            t2_z(OWN + a, o).start()
         return carry
 
-    lax.fori_loop(0, GROUPS, to_z, 0)
-    loads[2].wait()
-    merge(2)
+    lax.fori_loop(0, OWN, hand_on, 0)
+    lax.fori_loop(0, OWN, hand_on_other, 0)
 
     mine_a = pl.ds(pl.multiple_of(ROWS_A * k, PACK), ROWS_A)
     mine_a0 = pl.ds(pl.multiple_of(ROWS_A * k, PACK), CUT_A)
@@ -197,6 +222,15 @@
     mine_b = pl.ds(pl.multiple_of(BASE_B + ROWS_B * k, PACK), ROWS_B)
     theirs_b = pl.ds(pl.multiple_of(BASE_B + ROWS_B * (1 - k), PACK), ROWS_B)
     all_b = pl.ds(BASE_B, FULL_B)
+    back_a = pl.ds(pl.multiple_of(BACK_A * k, PACK), BACK_A)
+    back_a0 = pl.ds(pl.multiple_of(BACK_A * k, PACK), CUT_BACK)
+    back_a1 = pl.ds(pl.multiple_of(BACK_A * k + CUT_BACK, PACK), BACK_A - CUT_BACK)
+    swap = pl.ds(pl.multiple_of(BASE_BACK + BACK_B * k, PACK), SWAP)
+    rest = pl.ds(pl.multiple_of(BASE_BACK + BACK_B * k + SWAP, PACK), ROWS_B)
+    back_b = pl.ds(pl.multiple_of(BASE_BACK + BACK_B * k, PACK), BACK_B)
+    all_back = pl.ds(BASE_BACK, FULL_BACK)
+    back_b0 = pl.ds(BASE_BACK, BACK_B)
+    back_b1 = pl.ds(BASE_BACK + BACK_B, BACK_B)
     b0 = pl.ds(BASE_B, ROWS_B)
     b1 = pl.ds(BASE_B + ROWS_B, ROWS_B)
 
@@ -211,11 +245,11 @@
             lambda: cp(2, p.at[q, xo, :, mine_a1, :], ra2b.at[q], left),
             lambda: cp(3, p.at[q, xp, :, mine_a, :], ra3.at[q, 0], right),
             lambda: cp(4, p.at[q, xm, :, mine_a, :], ra3.at[q, 1], left),
-            lambda: same(5, h.at[q, xi, :, mine_a, :], right),
-            lambda: same(6, h.at[q, xi, :, mine_a, :], left),
-            lambda: same(7, h.at[q, xm, :, mine_a1, :], right),
-            lambda: same(8, h.at[q, xp, :, mine_a0, :], left),
-            lambda: same(9, h.at[q, :, :, mine_a, :], across),
+            lambda: same(5, h.at[q, xi, :, back_a, :], right),
+            lambda: same(6, h.at[q, xi, :, back_a, :], left),
+            lambda: same(7, h.at[q, xm, :, back_a1, :], right),
+            lambda: same(8, h.at[q, xp, :, back_a0, :], left),
+            lambda: same(9, h.at[q, :, :, back_a, :], across),
         ][which]()
 
     def b_copy(q, which):
@@ -229,18 +263,19 @@
             lambda: cp(2, p.at[q, xp, :, all_b, :], rb2.at[q, 0], right),
             lambda: cp(3, p.at[q, xm, :, all_b, :], rb2.at[q, 1], left),
             lambda: cp(4, p.at[q, xi, :, theirs_b, :], rb3.at[q], across),
-            lambda: same(5, h.at[q, xi, :, mine_b, :], across),
-            lambda: same(6, h.at[q, xi, :, all_b, :], right),
-            lambda: same(7, h.at[q, xi, :, all_b, :], left),
-            lambda: same(8, h.at[q, xm, :, b0, :], right),
-            lambda: same(9, h.at[q, xp, :, b1, :], left),
+            lambda: same(5, h.at[q, xi, :, back_b, :], across),
+            lambda: same(6, h.at[q, xi, :, all_back, :], right),
+            lambda: same(7, h.at[q, xi, :, all_back, :], left),
+            lambda: same(8, h.at[q, xm, :, back_b0, :], right),
+            lambda: same(9, h.at[q, xp, :, back_b1, :], left),
         ][which]()
 
     def add(ref, at, other):
         ref[at] = (ref[at].astype(F32) + other.astype(F32)).astype(BF16)
 
-    def matrix(i, s):
-        return x[i, s].reshape(SEGLEN, DS)
+    def matrix(i, q, seg):
+        first, which = group(q)
+        return x[i, first + seg, which].reshape(SEGLEN, DS)
 
     def spread(q):
         for o in range(1, NZ):
@@ -250,12 +285,14 @@
     def forward(q):
         t2_twin(q).wait_recv()
         for seg in range(2):
-            s = 2 * q + seg
-            xs, dys = matrix(0, s), matrix(1, s)
+            s = segment(q, seg)
+            xs, dys = matrix(0, q, seg), matrix(1, q, seg)
             for i, rows in enumerate((xs, xs, dys)):
                 part = dims(m[i, s], rows, 1, 1).astype(BF16)
                 for j in range(2):
-                    p[q, 2 * seg + j, i] = part[:, j * LANES : (j + 1) * LANES]
+                    half = part[:, j * LANES : (j + 1) * LANES]
+                    for place, unit, count in PLACES:
+                        p[q, 2 * seg + j, i, place : place + count] = half[unit : unit + count]
         a_copy(q, 0).start()
         b_copy(q, 0).start()
         b_copy(q, 1).start()
@@ -293,13 +330,16 @@
         p[at] = (p[at].astype(F32) + rb2[q, 0].astype(F32) + rb2[q, 1].astype(F32)).astype(BF16)
         cps(4).start()
 
-    def activate(q, rows, gud):
+    def activate(q, gud, *spans):
         g, u, dh = gud
         sig = jax.nn.sigmoid(g)
         act = g * sig
-        h[q, xi, 0, rows, :] = (dh * u * sig * (1.0 + g * (1.0 - sig))).astype(BF16)
-        h[q, xi, 1, rows, :] = (dh * act).astype(BF16)
-        h[q, xi, 2, rows, :] = (act * u).astype(BF16)
+        made = (dh * u * sig * (1.0 + g * (1.0 - sig)), dh * act, act * u)
+        for i, part in enumerate(made):
+            first = 0
+            for span in spans:
+                h[q, xi, i, span, :] = part[first : first + span.size].astype(BF16)
+                first += span.size
 
     def ea(q):
         cps = lambda i: a_copy(q, i)
@@ -307,20 +347,21 @@
         cps(4).wait_recv()
         activate(
             q,
-            mine_a,
             [
                 p[q, xi, i, mine_a, :].astype(F32) + ra3[q, 0, i].astype(F32) + ra3[q, 1, i].astype(F32)
                 for i in range(3)
             ],
+            back_a,
+            swap,
         )
+        b_copy(q, 5).start()
         cps(5).start()
         cps(6).start()
 
     def eb(q):
         cps = lambda i: b_copy(q, i)
         cps(4).wait_recv()
-        activate(q, mine_b, [p[q, xi, i, mine_b, :].astype(F32) + rb3[q, i].astype(F32) for i in range(3)])
-        cps(5).start()
+        activate(q, [p[q, xi, i, mine_b, :].astype(F32) + rb3[q, i].astype(F32) for i in range(3)], rest)
 
     def a5(q):
         cps = lambda i: a_copy(q, i)
@@ -348,9 +389,9 @@
         cps(7).wait_recv()
         cps(9).start()
 
-    def keep(q):
-        pair = pl.ds(2 * q, 2)
-        return pltpu.make_async_copy(m.at[:, pair], grad_out.at[:, pair], pw.at[q])
+    def keep(q, seg):
+        s = segment(q, seg)
+        return pltpu.make_async_copy(m.at[:, s], grad_out.at[:, s], pw.at[seg, q])
 
     def d_copy(q, i):
         def cp(src, dst, dev):
@@ -359,7 +400,7 @@
         if i == 0:
             return cp(dx.at[q, :, :, 1 - c], dxc.at[q], twin)
         if i == 4:
-            return cp(dy.at[q], ry.at[q], high)
+            return remote(dy.at[q], ry.at[q], d_s.at[i, q], d_r.at[i, q], high)
         return cp(dz.at[q, :, lax.rem(z + i, NZ)], rz.at[q, i - 1], along_z(i))
 
     def grads(q):
@@ -368,7 +409,7 @@
         b_copy(q, 9).wait_recv()
         parts = []
         for seg in range(2):
-            s = 2 * q + seg
+            s = segment(q, seg)
             dg, du, hh = (
                 jnp.concatenate([h[q, 2 * seg, i], h[q, 2 * seg + 1, i]], axis=1) for i in range(3)
             )
@@ -377,13 +418,13 @@
             parts.append((dg, du, hh))
         d_copy(q, 0).start()
         for seg in range(2):
-            s = 2 * q + seg
+            s = segment(q, seg)
             dg, du, hh = parts[seg]
-            xs, dys = matrix(0, s), matrix(1, s)
+            xs, dys = matrix(0, q, seg), matrix(1, q, seg)
             m[0, s] = nn(dg, xs).astype(BF16)
             m[1, s] = nn(du, xs).astype(BF16)
             m[2, s] = nn(hh, dys).astype(BF16)
-        keep(q).start()
+            keep(q, seg).start()
 
     def d2(q):
         cps = lambda i: d_copy(q, i)
@@ -399,34 +440,42 @@
         for o in range(1, NZ):
             cps(o).wait_recv()
 
-        def part(which):
-            total = dx[q, which, z, c]
-            for o in range(NZ - 1):
-                total = total + rz[q, o, which].astype(F32)
-            return total
-
-        dy[q] = part(1 - yh).astype(BF16)
-        cps(4).start()
-        dx[q, yh, z, c] = part(yh)
-
-    def final(q, away):
-        o = lax.rem(q - d + GROUPS, GROUPS)
-        dst = outs.at[:, pl.ds(pl.multiple_of(d * DS, LANES), DS)]
+        total = dx[q, :, z, c]
+        for o in range(NZ - 1):
+            total = total + rz[q, o].astype(F32)
+
+        @pl.when(q >= OWN)
+        def _():
+            dy[q - OWN] = total.astype(BF16)
+            d_copy(q - OWN, 4).start()
+
+        @pl.when(q < OWN)
+        def _():
+            dx[q, :, z, c] = total
+
+    def final(dest, away):
+        o = lax.rem(dest - d + GROUPS, GROUPS)
+        src, dst = fo.at[dest], outs.at[:, pl.ds(pl.multiple_of(d * DS, LANES), DS)]
         if away:
-            return remote(fo.at[q], dst, f_s.at[o], f_r.at[o], (q, t))
-        return pltpu.make_async_copy(fo.at[q], dst, f_r.at[o])
+            return remote(src, dst, f_s.at[o], f_r.at[o], (dest, t))
+        return pltpu.make_async_copy(src, dst, f_r.at[o])
 
     def d4(q):
-        d_copy(q, 4).wait_recv()
-        fo[q] = (dx[q, yh, z, c] + ry[q].astype(F32)).astype(BF16)
-
-        @pl.when(q != d)
+        @pl.when(q >= OWN)
         def _():
-            final(q, True).start()
-
-        @pl.when(q == d)
-        def _():
-            final(q, False).start()
+            a = q - OWN
+            d_copy(a, 4).wait_recv()
+            for i in range(2):
+                dest = 2 * a + i
+                fo[dest] = (dx[a, i, z, c] + ry[a, i].astype(F32)).astype(BF16)
+
+                @pl.when(dest != d)
+                def _(dest=dest):
+                    final(dest, True).start()
+
+                @pl.when(dest == d)
+                def _(dest=dest):
+                    final(dest, False).start()
 
     stages = dict(
         spread=spread, forward=forward, a2=a2, b2=b2, a3=a3, b3=b3, ea=ea, eb=eb, a5=a5, b5=b5,
@@ -458,13 +507,12 @@
 
         lax.fori_loop(0, FS // PACK, step, 0, unroll=11)
 
+    last = jnp.int32(GROUPS - 1)
     inner(0)
-    d2(GROUPS - 1)
-    d3(GROUPS - 2)
-    d4(GROUPS - 3)
+    d2(last)
+    d3(last - 1)
+    d4(last - 2)
     inner(1)
-    d3(GROUPS - 1)
-    d4(GROUPS - 2)
     inner(2)
     square = gsum.shape
     row = lax.broadcasted_iota(jnp.int32, square, 0)
@@ -487,12 +535,44 @@
     art[t] = own
     for o in range(1, NT):
         r_copy(o).start()
-    d4(GROUPS - 1)
+    d3(last)
+    d4(last - 1)
+
+    def drain(q, carry):
+        for i in range(10):
+            a_copy(q, i).wait_send()
+            b_copy(q, i).wait_send()
+        return carry
+
+    lax.fori_loop(0, GROUPS, drain, 0)
     for o in range(1, NT):
         r_copy(o).wait_recv()
     ard[d] = jnp.sum(art[...], axis=0)
     for o in range(1, GROUPS):
         r_copy(NT + o - 1).start()
+    d4(last)
+
+    def drain_rest(q, carry):
+        for o in range(1, NZ):
+            t2_z(q, o).wait_send()
+            d_copy(q, o).wait_send()
+        t2_twin(q).wait_send()
+        d_copy(q, 0).wait_send()
+        for seg in range(2):
+            keep(q, seg).wait()
+
+        @pl.when(q < OWN)
+        def _():
+            t2_high(q).wait_send()
+            d_copy(q, 4).wait_send()
+
+        return carry
+
+    lax.fori_loop(0, GROUPS, drain_rest, 0)
+    for o in range(1, GROUPS):
+        t1_copy(o).wait_send()
+    for o in range(1, NT):
+        r_copy(o).wait_send()
     for o in range(1, GROUPS):
         r_copy(NT + o - 1).wait_recv()
     total = ((ard[0] + ard[1]) + (ard[2] + ard[3])) + ((ard[4] + ard[5]) + (ard[6] + ard[7]))
@@ -502,31 +582,17 @@
         ref = outs.at[:, pl.ds(0, DS)]
         pltpu.make_async_copy(ref, ref, f_r.at[o]).wait()
     dx_out[...] = outs[...]
-    for i in range(1, NT + GROUPS - 1):
-        r_copy(i).wait_send()
     for o in range(1, GROUPS):
-        for copy in t1_copies(o):
-            copy.wait_send()
-
-    def drain(q, carry):
-        t2_high(q).wait_send()
-        for o in range(1, NZ):
-            t2_z(q, o).wait_send()
-        t2_twin(q).wait_send()
-        for i in range(10):
-            a_copy(q, i).wait_send()
-            b_copy(q, i).wait_send()
-        for i in range(5):
-            d_copy(q, i).wait_send()
-        keep(q).wait()
-
+        r_copy(NT + o - 1).wait_send()
+
+    def drain_final(q, carry):
         @pl.when(q != d)
         def _():
             final(q, True).wait_send()
 
         return carry
 
-    lax.fori_loop(0, GROUPS, drain, 0)
+    lax.fori_loop(0, GROUPS, drain_final, 0)
 
 
 def run_layer(tokens, cotangent, w_gate, w_up, w_down, router):
@@ -536,7 +602,8 @@
     n = GROUPS
     stacked = (3, SEGS, FS, DS)
     scratch = [
-        vm((2, SEGS, NZ, 2, BLOCK, DS), BF16),
+        vm((2, BLOCK, n * DS), BF16), vm((SEGS, EXPERTS), F32),
+        vm((2, n, 2, NZ, 2, BLOCK, DS), BF16),
         vm((3, EXPERTS, FS, DS), BF16), vm(stacked, BF16),
         vm((DS, DS), BF16), vm((DS, DS), BF16),
         vm((n, NX, 3, FS, LANES), BF16), vm((n, NX, 3, FS, LANES), BF16),
@@ -546,13 +613,13 @@
         vm((n, 2, 3, ROWS_B, LANES), BF16), vm((n, 2, 3, FULL_B, LANES), BF16), vm((n, 3, ROWS_B, LANES), BF16),
         vm((n, 2, NZ, 2, BLOCK, DS), F32), vm((n, 2, NZ, BLOCK, DS), F32),
         vm((n, 2, NZ, BLOCK, DS), BF16), vm((n, NZ - 1, 2, BLOCK, DS), BF16),
-        vm((n, BLOCK, DS), BF16), vm((n, BLOCK, DS), BF16), vm((n, BLOCK, DS), BF16),
+        vm((OWN, 2, BLOCK, DS), BF16), vm((OWN, 2, BLOCK, DS), BF16), vm((n, BLOCK, DS), BF16),
         vm((BLOCK, n * DS), BF16),
         vm((DS, DS), F32),
         vm((NT, SEGS, LANES), F32), vm((n, SEGS, LANES), F32),
-        dma((3,)), dma((2, n)), dma((2, n)), dma((5, n)), dma((5, n)),
+        dma((6,)), dma((n,)), dma((n,)), dma((5, n)), dma((5, n)),
         dma((10, n)), dma((10, n)), dma((10, n)), dma((10, n)),
-        dma((5, n)), dma((5, n)), dma((n,)), dma((n,)), dma((n,)), dma((NT + n - 1,)), dma((NT + n - 1,)),
+        dma((5, n)), dma((5, n)), dma((n,)), dma((n,)), dma((2, n)), dma((NT + n - 1,)), dma((NT + n - 1,)),
     ]
     return pl.pallas_call(
         layer_kernel,
@@ -561,7 +628,7 @@
             jax.ShapeDtypeStruct((SEGS, EXPERTS), F32),
             jax.ShapeDtypeStruct(stacked, BF16),
         ),
-        in_specs=[vm_spec, vm_spec, vm_spec, any_spec, any_spec, any_spec],
+        in_specs=[any_spec] * 6,
         out_specs=[vm_spec, vm_spec, any_spec],
         scratch_shapes=scratch,
         compiler_params=pltpu.CompilerParams(

time: 176 us -> 172 us (0.977)
  Pallas kernels: 175 us -> 171 us
    pallas_call x1, Pallas kernels: 166 us -> 162 us  [run_layer(): pl.pallas_call(layer_kernel, out_shape=(jax.ShapeDtypeStruct((BLOCK, n *...]
where the time goes in v3:
time: 172 us
  Pallas kernels  171 us (99%)
    pallas_call x1, Pallas kernels, run_layer(): pl.pallas_call(layer_kernel, out_shape=(jax.ShapeDtypeStruct((BLOCK, n *...  162 us
    pallas_call x1, Pallas kernels, combine(): pl.pallas_call(combine_kernel, out_shape=[jax.ShapeDtypeStruct((EXPERTS,...  9.21 us

profile of v3, /device:TPU:1, one launch (start us, length us, event | category | flops | bytes accessed | tf_op | source)
XLA Modules:
  0.0 171.5 jit_solution(10850798468040949828)
XLA Ops:
  0.6 161.5 %layer_backward.1 = (bf16[32,2048]{1,0:T(8,128)(2,1)}, f32[16,16]{1,0:T(8,128)}, bf16[3,16,352,256]{3,2,1,0:T(8,128)(2,1)}) custom-call(bf16[32,2048]{1,0:T(8,128)(2,1)} %tok_in.1, bf16[32,2048]{1,0:T(8,128)(2,1)} %cot_in.1, f32[16,16]{1,0:T(8,128)} %router.1, bf16[16,352,256]{2,1,0:T(8,128)(2,1)} %bitcast.4, bf16[16,352,256]{2,1,0:T(8,128)(2,1)} %bitcast.5, ...), custom_call_target="tpu_custom_call" | custom-call | tf_op jit(solution)/shard_map/layer_backward/pallas_call | solution.py:624
  162.2 9.2 %combine_experts.1 = (bf16[16,352,256]{2,1,0:T(8,128)(2,1)}, bf16[16,352,256]{2,1,0:T(8,128)(2,1)}, bf16[16,352,256]{2,1,0:T(8,128)(2,1)}, bf16[32,2048]{1,0:T(8,128)(2,1)}, f32[16,16]{1,0:T(8,128)}) custom-call(f32[16,16]{1,0:T(8,128)} %router.1, bf16[3,16,352,256]{3,2,1,0:T(8,128)(2,1)} %get-tuple-element.13.src, ...), custom_call_target="tpu_custom_call" | custom-call | tf_op jit(solution)/shard_map/combine_experts/pallas_call | solution.py:676

commit v4 on v3

--- a/solution.py
+++ b/solution.py
@@ -46,11 +46,11 @@
 PACK = 16
 
 ORDER = (
-    ("spread", -1),
     ("b3", 6),
     ("a2", 3),
     ("grads", 13),
     ("forward", 0),
+    ("spread", -1),
     ("a6", 11),
     ("a5", 10),
     ("eb", 8),
@@ -62,6 +62,7 @@
     ("d2", 14),
     ("d3", 15),
     ("d4", 16),
+    ("settle", 16),
 )
 LAST = 13
 TICKS = GROUPS + LAST
@@ -105,12 +106,15 @@
     t = lax.axis_index("tensor")
     xi, k = d // 2, d % 2
     yh, z, c = t // 8, (t // 2) % NZ, t % 2
-    right = (lax.rem(xi + 1, NX) * 2 + k, t)
-    left = (lax.rem(xi + 3, NX) * 2 + k, t)
     across = (xi * 2 + 1 - k, t)
     high = (d, (1 - yh) * 8 + z * 2 + c)
     twin = (d, yh * 8 + z * 2 + 1 - c)
-    xp, xm, xo = lax.rem(xi + 1, NX), lax.rem(xi + 3, NX), lax.rem(xi + 2, NX)
+    xo = lax.rem(xi + 2, NX)
+
+    def sides(q):
+        turn = 2 * lax.rem(q, 2)
+        xp, xm = lax.rem(xi + 1 + turn, NX), lax.rem(xi + 3 + turn, NX)
+        return (xp * 2 + k, t), (xm * 2 + k, t), xp, xm
 
     def along_z(o):
         return (d, yh * 8 + lax.rem(z + o, NZ) * 2 + c)
@@ -235,6 +239,8 @@
     b1 = pl.ds(BASE_B + ROWS_B, ROWS_B)
 
     def a_copy(q, which):
+        right, left, xp, xm = sides(q)
+
         def cp(i, src, dst, dev):
             return remote(src, dst, a_s.at[i, q], a_r.at[i, q], dev)
 
@@ -253,6 +259,8 @@
         ][which]()
 
     def b_copy(q, which):
+        right, left, xp, xm = sides(q)
+
         def cp(i, src, dst, dev):
             return remote(src, dst, b_s.at[i, q], b_r.at[i, q], dev)
 
@@ -305,6 +313,7 @@
         cps(2).start()
 
     def b2(q):
+        xp, xm = sides(q)[2:]
         cps = lambda i: b_copy(q, i)
         cps(0).wait_recv()
         add(p, (q, xp, slice(None), b0, slice(None)), rb1[q, 0])
@@ -314,6 +323,7 @@
         cps(3).start()
 
     def a3(q):
+        xp, xm = sides(q)[2:]
         cps = lambda i: a_copy(q, i)
         cps(1).wait_recv()
         add(p, (q, xp, slice(None), mine_a0, slice(None)), ra2a[q])
@@ -477,7 +487,20 @@
                 def _(dest=dest):
                     final(dest, False).start()
 
+    def settle(q):
+        for i in range(10):
+            a_copy(q, i).wait_send()
+            b_copy(q, i).wait_send()
+        for o in range(1, NZ):
+            t2_z(q, o).wait_send()
+            d_copy(q, o).wait_send()
+        t2_twin(q).wait_send()
+        d_copy(q, 0).wait_send()
+        for seg in range(2):
+            keep(q, seg).wait()
+
     stages = dict(
+        settle=settle,
         spread=spread, forward=forward, a2=a2, b2=b2, a3=a3, b3=b3, ea=ea, eb=eb, a5=a5, b5=b5,
         a6=a6, b6=b6, grads=grads, d2=d2, d3=d3, d4=d4,
     )
@@ -538,13 +561,6 @@
     d3(last)
     d4(last - 1)
 
-    def drain(q, carry):
-        for i in range(10):
-            a_copy(q, i).wait_send()
-            b_copy(q, i).wait_send()
-        return carry
-
-    lax.fori_loop(0, GROUPS, drain, 0)
     for o in range(1, NT):
         r_copy(o).wait_recv()
     ard[d] = jnp.sum(art[...], axis=0)
@@ -552,23 +568,10 @@
         r_copy(NT + o - 1).start()
     d4(last)
 
-    def drain_rest(q, carry):
-        for o in range(1, NZ):
-            t2_z(q, o).wait_send()
-            d_copy(q, o).wait_send()
-        t2_twin(q).wait_send()
-        d_copy(q, 0).wait_send()
-        for seg in range(2):
-            keep(q, seg).wait()
-
-        @pl.when(q < OWN)
-        def _():
-            t2_high(q).wait_send()
-            d_copy(q, 4).wait_send()
-
-        return carry
-
-    lax.fori_loop(0, GROUPS, drain_rest, 0)
+    lax.fori_loop(GROUPS - 3, GROUPS, lambda q, carry: settle(q) or carry, 0)
+    for a in range(OWN):
+        t2_high(a).wait_send()
+        d_copy(a, 4).wait_send()
     for o in range(1, GROUPS):
         t1_copy(o).wait_send()
     for o in range(1, NT):

time: 172 us -> 170 us (0.988)
  Pallas kernels: 171 us -> 169 us
where the time goes in v4:
time: 170 us
  Pallas kernels  169 us (99%)
    pallas_call x1, Pallas kernels, run_layer(): pl.pallas_call(layer_kernel, out_shape=(jax.ShapeDtypeStruct((BLOCK, n *...  160 us
    pallas_call x1, Pallas kernels, combine(): pl.pallas_call(combine_kernel, out_shape=[jax.ShapeDtypeStruct((EXPERTS,...  9.21 us

profile of v4, /device:TPU:1, one launch (start us, length us, event | category | flops | bytes accessed | tf_op | source)
XLA Modules:
  0.0 169.8 jit_solution(16129687349153415521)
XLA Ops:
  0.6 159.8 %layer_backward.1 = (bf16[32,2048]{1,0:T(8,128)(2,1)}, f32[16,16]{1,0:T(8,128)}, bf16[3,16,352,256]{3,2,1,0:T(8,128)(2,1)}) custom-call(bf16[32,2048]{1,0:T(8,128)(2,1)} %tok_in.1, bf16[32,2048]{1,0:T(8,128)(2,1)} %cot_in.1, f32[16,16]{1,0:T(8,128)} %router.1, bf16[16,352,256]{2,1,0:T(8,128)(2,1)} %bitcast.4, bf16[16,352,256]{2,1,0:T(8,128)(2,1)} %bitcast.5, ...), custom_call_target="tpu_custom_call" | custom-call | tf_op jit(solution)/shard_map/layer_backward/pallas_call | solution.py:627
  160.5 9.2 %combine_experts.1 = (bf16[16,352,256]{2,1,0:T(8,128)(2,1)}, bf16[16,352,256]{2,1,0:T(8,128)(2,1)}, bf16[16,352,256]{2,1,0:T(8,128)(2,1)}, bf16[32,2048]{1,0:T(8,128)(2,1)}, f32[16,16]{1,0:T(8,128)}) custom-call(f32[16,16]{1,0:T(8,128)} %router.1, bf16[3,16,352,256]{3,2,1,0:T(8,128)(2,1)} %get-tuple-element.13.src, ...), custom_call_target="tpu_custom_call" | custom-call | tf_op jit(solution)/shard_map/combine_experts/pallas_call | solution.py:679

commit v5 on v4

--- a/solution.py
+++ b/solution.py
@@ -48,6 +48,10 @@
 ORDER = (
     ("b3", 6),
     ("a2", 3),
+    ("d2", 14),
+    ("d3", 15),
+    ("d4", 16),
+    ("settle", 16),
     ("grads", 13),
     ("forward", 0),
     ("spread", -1),
@@ -59,10 +63,6 @@
     ("b5", 10),
     ("a3", 4),
     ("b6", 11),
-    ("d2", 14),
-    ("d3", 15),
-    ("d4", 16),
-    ("settle", 16),
 )
 LAST = 13
 TICKS = GROUPS + LAST
@@ -534,8 +534,8 @@
     inner(0)
     d2(last)
     d3(last - 1)
+    inner(1)
     d4(last - 2)
-    inner(1)
     inner(2)
     square = gsum.shape
     row = lax.broadcasted_iota(jnp.int32, square, 0)

time: 170 us -> 167 us (0.982)
  Pallas kernels: 169 us -> 166 us
    pallas_call x1, Pallas kernels: 160 us -> 157 us  [run_layer(): pl.pallas_call(layer_kernel, out_shape=(jax.ShapeDtypeStruct((BLOCK, n *...]
where the time goes in v5:
time: 167 us
  Pallas kernels  166 us (99%)
    pallas_call x1, Pallas kernels, run_layer(): pl.pallas_call(layer_kernel, out_shape=(jax.ShapeDtypeStruct((BLOCK, n *...  157 us
    pallas_call x1, Pallas kernels, combine(): pl.pallas_call(combine_kernel, out_shape=[jax.ShapeDtypeStruct((EXPERTS,...  9.22 us

profile of v5, /device:TPU:1, one launch (start us, length us, event | category | flops | bytes accessed | tf_op | source)
XLA Modules:
  0.0 167.2 jit_solution(532216993552657906)
XLA Ops:
  0.6 157.2 %layer_backward.1 = (bf16[32,2048]{1,0:T(8,128)(2,1)}, f32[16,16]{1,0:T(8,128)}, bf16[3,16,352,256]{3,2,1,0:T(8,128)(2,1)}) custom-call(bf16[32,2048]{1,0:T(8,128)(2,1)} %tok_in.1, bf16[32,2048]{1,0:T(8,128)(2,1)} %cot_in.1, f32[16,16]{1,0:T(8,128)} %router.1, bf16[16,352,256]{2,1,0:T(8,128)(2,1)} %bitcast.4, bf16[16,352,256]{2,1,0:T(8,128)(2,1)} %bitcast.5, ...), custom_call_target="tpu_custom_call" | custom-call | tf_op jit(solution)/shard_map/layer_backward/pallas_call | solution.py:627
  157.8 9.2 %combine_experts.1 = (bf16[16,352,256]{2,1,0:T(8,128)(2,1)}, bf16[16,352,256]{2,1,0:T(8,128)(2,1)}, bf16[16,352,256]{2,1,0:T(8,128)(2,1)}, bf16[32,2048]{1,0:T(8,128)(2,1)}, f32[16,16]{1,0:T(8,128)}) custom-call(f32[16,16]{1,0:T(8,128)} %router.1, bf16[3,16,352,256]{3,2,1,0:T(8,128)(2,1)} %get-tuple-element.13.src, ...), custom_call_target="tpu_custom_call" | custom-call | tf_op jit(solution)/shard_map/combine_experts/pallas_call | solution.py:679
